TPU v7x, 32 devices: a whole 2x2x4 slice. The times are simulated.
32 devices in a mesh: row: 8 (over y, x, core), col: 4 (over z).
Axes of the slice: x: 2, y: 2, z: 4, core: 2. Of those that a mesh axis runs over, the one named last changes fastest.
Arguments:
- confidence: bfloat16 [512, 128, 128], P(('row', 'col')), as said below
- item_blocks: int32 [512], P(('row', 'col')), may hold values from 0 to 3
- counts: int32 [256], P(('row', 'col')), may hold values from 0 to 2, as said below
- item_factors: bfloat16 [4096, 128], P(('row', 'col')), may hold values from -0.3125 to 0.3125
Outputs:
- solution: float32 [4096, 128], P(('row', 'col'))
- residual: float32 [4096, 128], P(('row', 'col'))
Inputs may be any that keep to these rules, and one draw needn't show every extreme that they name: `counts`: every device has some owner row with all 2 slots live. `confidence`: entries are non-negative; about half of them are zero.
All inputs are finite; a program needn't handle non-finite values.
Results may differ from a plain program's by a relative error of at most 0.035.
Values may be sent and summed in bfloat16 or wider, within the bound.
No kernel may reach another device: no remote copies, remote signals or barrier semaphores. Data moves between devices by JAX's collectives and lax.ppermute only.
A program may use at most 64 MiB of HBM per device.

v0:
```python
import jax
import jax.numpy as jnp
from jax import lax
from jax.sharding import PartitionSpec as P

ITERS = 2


ridge = 2.0


def shards(confidence, item_blocks, counts, item_factors):
    slots = confidence.shape[0]
    width = confidence.shape[1]
    factor_width = item_factors.shape[1]
    groups = lax.axis_size("row")
    per_owner = slots // groups
    active = jnp.arange(slots) % per_owner < jnp.repeat(counts, per_owner)
    weights = confidence * active.astype(confidence.dtype)[:, None, None]
    weights = weights.reshape(groups, per_owner, width, width)
    slab = lax.all_gather(item_factors, "col", axis=0, tiled=True)
    picked = slab.reshape(-1, width, factor_width)[item_blocks]
    tiles = picked.reshape(groups, per_owner, width, factor_width)

    def regroup(user_rows):
        rounded = user_rows.astype(jnp.bfloat16)
        flat = rounded.reshape(groups * width, factor_width)
        arrived = lax.all_to_all(flat, "row", split_axis=0, concat_axis=0, tiled=True)
        return jnp.sum(arrived.reshape(groups, width, factor_width).astype(jnp.float32), axis=0)

    def squared_norm(vector):
        return lax.psum(jnp.sum(vector * vector), ("row", "col"))

    rhs = regroup(jnp.einsum("gcui,gcik->guk", weights, tiles, preferred_element_type=jnp.float32))
    solution = jnp.zeros_like(rhs)
    residual = rhs
    direction = rhs
    norm_now = squared_norm(residual)
    for iteration in range(ITERS):
        dirs_low = direction.astype(jnp.bfloat16)
        gathered = lax.all_gather(dirs_low, "row", axis=0, tiled=True)
        dir_groups = gathered.reshape(groups, width, factor_width)
        scores = jnp.einsum("guk,gcik->gcui", dir_groups, tiles, preferred_element_type=jnp.float32)
        weighted = (weights * scores).astype(jnp.bfloat16)
        apply_user_rows = jnp.einsum(
            "gcui,gcik->guk", weighted, tiles, preferred_element_type=jnp.float32
        )
        image = ridge * direction + regroup(apply_user_rows)
        step_size = norm_now / lax.psum(jnp.sum(direction * image), ("row", "col"))
        solution = solution + step_size * direction
        residual = residual - step_size * image
        if iteration + 1 < ITERS:
            norm_next = squared_norm(residual)
            direction = residual + norm_next / norm_now * direction
            norm_now = norm_next
    return (solution, residual)


def solution(mesh):
    return jax.shard_map(
        shards,
        mesh=mesh,
        in_specs=(
            P(("row", "col"), None, None),
            P(("row", "col")),
            P(("row", "col")),
            P(("row", "col"), None),
        ),
        out_specs=(P(("row", "col"), None), P(("row", "col"), None)),
        check_vma=False,
    )
```

profile of v0, /device:TPU:0, one launch (start us, length us, event | category | flops | bytes accessed | tf_op | source)
XLA Modules:
  0.0 193.1 jit_solution(12996219279855217030)
XLA Ops:
  0.6 0.7 compare_select_fusion
  1.3 0.0 copy-start.1
  1.3 0.6 copy-done.1
  1.9 0.1 broadcast_in_dim.7
  2.0 0.1 reshape.55
  2.1 15.3 %all_gather.9 = bf16[512,128]{1,0:T(8,128)(2,1)S(1)} all-gather(bf16[128,128]{1,0:T(8,128)(2,1)} %param.7), channel_id=1, replica_groups=mesh['row'=8,'col'=4] {'col'}, dimensions={0}, use_global_device_ids=true | all-gather | bytes 163840 | tf_op jit(solution)/shard_map/all_gather | solution.py:21
  17.4 0.0 copy-start
  17.4 0.6 gather_fusion
  18.0 0.4 copy-done
  18.4 0.1 broadcast_multiply_fusion
  18.5 0.3 fusion.8
  18.8 10.5 %all_to_all.18 = bf16[8,128,128]{2,1,0:T(8,128)(2,1)S(1)} all-to-all(bf16[8,128,128]{2,1,0:T(8,128)(2,1)S(1)} %fusion.8), channel_id=1, replica_groups=mesh['row'=8,'col'=4] {'row'}, dimensions={0} | all-to-all | bytes 524288 | tf_op jit(solution)/shard_map/all_to_all | solution.py:28
  29.3 8.4 %all_gather.10 = bf16[1024,128]{1,0:T(8,128)(2,1)S(1)} all-gather(bf16[128,128]{1,0:T(8,128)(2,1)S(1)} %convert_element_type.45), channel_id=1, replica_groups=mesh['row'=8,'col'=4] {'row'}, dimensions={0}, use_global_device_ids=true | all-gather | bytes 294912 | tf_op jit(solution)/shard_map/all_gather | solution.py:41
  37.7 0.4 fusion.9
  38.1 9.5 %all_to_all.19 = bf16[8,128,128]{2,1,0:T(8,128)(2,1)S(1)} all-to-all(bf16[8,128,128]{2,1,0:T(8,128)(2,1)S(1)} %fusion.9), channel_id=1, replica_groups=mesh['row'=8,'col'=4] {'row'}, dimensions={0} | all-to-all | bytes 524288 | tf_op jit(solution)/shard_map/all_to_all | solution.py:28
  47.6 0.6 multiply_reduce_fusion.2
  48.3 39.8 %all-reduce = (f32[]{:T(128)}, f32[]{:T(128)}) all-reduce(f32[]{:T(128)} %get-tuple-element.3, f32[]{:T(128)} %get-tuple-element.2), channel_id=1, replica_groups=mesh['row'=8,'col'=4] {'row','col'}, use_global_device_ids=true, to_apply=%region_2.3 | all-reduce | flops 2 | bytes 16 | tf_op jit(solution)/shard_map/psum | solution.py:32
  89.4 0.6 multiply_reduce_fusion.1
  90.0 40.6 %psum.30 = f32[]{:T(128)} all-reduce(f32[]{:T(128)} %multiply_reduce_fusion.1), channel_id=1, replica_groups=mesh['row'=8,'col'=4] {'row','col'}, use_global_device_ids=true, to_apply=%region_7.8 | all-reduce | flops 1 | bytes 8 | tf_op jit(solution)/shard_map/psum | solution.py:32
  132.0 10.3 %all_gather.11 = bf16[1024,128]{1,0:T(8,128)(2,1)S(1)} all-gather(bf16[128,128]{1,0:T(8,128)(2,1)S(1)} %fusion.11), channel_id=1, replica_groups=mesh['row'=8,'col'=4] {'row'}, dimensions={0}, use_global_device_ids=true | all-gather | bytes 294912 | tf_op jit(solution)/shard_map/all_gather | solution.py:41
  142.3 0.4 fusion.10
  142.7 9.5 %all_to_all.20 = bf16[8,128,128]{2,1,0:T(8,128)(2,1)S(1)} all-to-all(bf16[8,128,128]{2,1,0:T(8,128)(2,1)S(1)} %fusion.10), channel_id=1, replica_groups=mesh['row'=8,'col'=4] {'row'}, dimensions={0} | all-to-all | bytes 524288 | tf_op jit(solution)/shard_map/all_to_all | solution.py:28
  152.2 0.6 multiply_reduce_fusion
  152.8 38.3 %psum.31 = f32[]{:T(128)} all-reduce(f32[]{:T(128)} %multiply_reduce_fusion), channel_id=1, replica_groups=mesh['row'=8,'col'=4] {'row','col'}, use_global_device_ids=true, to_apply=%region_10.11 | all-reduce | flops 1 | bytes 8 | tf_op jit(solution)/shard_map/psum | solution.py:49
  192.4 0.7 multiply_subtract_fusion
  (7 shorter events, 0.2 us)
Async XLA Ops:
  1.3 0.7 copy-start.1
  17.4 1.0 copy-start
where the time goes:
time: 194 us; the launch traced here: 193 us
  blocking collectives  182 us (94%)
  between operations  4.72 us (2%)
  other arithmetic  3.47 us (2%)
    psum x2, blocking collectives, squared_norm(): return lax.psum(jnp.sum(vector * vector), ('row', 'col'))  80.4 us
    psum x1, blocking collectives, shards(): step_size = norm_now / lax.psum(jnp.sum(direction * image), ('row', 'col'))  38.3 us
    all_to_all x3, blocking collectives, regroup(): lax.all_to_all(flat, 'row', split_axis=0, concat_axis=0, tiled=True)  29.4 us
    all_gather x2, blocking collectives, shards(): gathered = lax.all_gather(dirs_low, 'row', axis=0, tiled=True)  18.6 us
    all_gather x1, blocking collectives, shards(): slab = lax.all_gather(item_factors, 'col', axis=0, tiled=True)  15.3 us

commit v1 on v0

v1 whole, which is shorter than its diff:
```python
import functools

import jax
import jax.numpy as jnp
from jax import lax
from jax.experimental import pallas as pl
from jax.experimental.pallas import tpu as pltpu
from jax.sharding import PartitionSpec as P

ridge = 2.0
VMEM_LIMIT = 48 * 1024 * 1024
BB, BQ, VV, VB, VU, CROSS, STEP = range(7)


def dot(a, b, contract):
    return lax.dot_general(a, b, ((contract[:1], contract[1:]), ((), ())), preferred_element_type=jnp.float32)


def total(a):
    return jnp.sum(a, axis=(0, 1), keepdims=True)


def load_kernel(confidence, item_blocks, counts, block, *refs):
    parcels, (blocks_here, counts_here, block_here, arrived) = refs[:-4], refs[-4:]
    groups = len(parcels)
    per_owner = confidence.shape[0] // groups
    row = lax.axis_index("row")
    pairs = [
        (confidence.at[pl.ds((row ^ shift) * per_owner, per_owner)], parcel.at[pl.ds(0, per_owner)])
        for shift, parcel in enumerate(parcels)
    ]
    pairs += [(item_blocks, blocks_here), (counts, counts_here), (block, block_here)]
    copies = [pltpu.make_async_copy(source, target, arrived.at[i]) for i, (source, target) in enumerate(pairs)]
    for copy in copies:
        copy.start()
    for copy in copies:
        copy.wait()


def pick_kernel(groups, cols, item_blocks, counts, *refs):
    blocks, parcels, slab = refs[:cols], refs[-1 - groups:-1], refs[-1]
    for shift, block in zip(col_order(cols), blocks):
        slab[shift] = block[...]
    row, col = lax.axis_index("row"), lax.axis_index("col")
    per_owner = item_blocks.shape[0] // groups
    for shift, parcel in enumerate(parcels):
        owner = row ^ shift
        first = parcel.shape[0] - per_owner
        for place in range(per_owner):
            tile = slab[item_blocks[owner * per_owner + place] ^ col]
            parcel[first + place] = jnp.where(place < counts[owner], tile, jnp.zeros_like(tile))


def krylov_kernel(whole, split, b_ref, q_ref, v_ref, u_ref, stats):
    factor_width = b_ref.shape[1]

    def tiles_of(weights, items):
        x = items[...].reshape(-1, factor_width)
        w = jnp.concatenate([weights[place] for place in range(weights.shape[0])], axis=1)
        return x, w

    def tiles():
        for parcel in whole:
            half = parcel.shape[0] // 2
            yield tiles_of(parcel.at[pl.ds(0, half)], parcel.at[pl.ds(half, half)])
        for weights, items in split:
            yield tiles_of(weights, items)

    def apply(field):
        low = field.astype(jnp.bfloat16)
        image = ridge * field
        for x, w in tiles():
            scores = dot(low, x, (1, 1))
            weighted = (w.astype(jnp.float32) * scores).astype(jnp.bfloat16)
            image = image + dot(weighted, x, (1, 0))
        return image

    b = jnp.zeros(b_ref.shape, jnp.float32)
    for x, w in tiles():
        b = b + dot(w, x, (1, 0))
    q = apply(b)
    bb, bq = total(b * b), total(b * q)
    step = jnp.where(bq > 0, bb / bq, 1.0)
    v = b - step * q
    u = apply(v)
    b_ref[...] = b
    q_ref[...] = q
    v_ref[...] = v
    u_ref[...] = u
    values = {
        BB: bb, BQ: bq, VV: total(v * v), VB: total(v * b),
        VU: total(v * u), CROSS: total(v * q + b * u), STEP: step,
    }
    lane = lax.broadcasted_iota(jnp.int32, stats.shape[1:], 1)
    packed = jnp.zeros(stats.shape[1:], jnp.float32)
    for place, value in values.items():
        packed = jnp.where(lane == place, value, packed)
    stats[0] = packed


def finish_kernel(every, own, b_ref, q_ref, v_ref, u_ref, solution_ref, residual_ref):
    def field(place):
        return every[:, 0, place:place + 1]

    norm_now = jnp.sum(field(BB), axis=0, keepdims=True)
    step_0 = norm_now / jnp.sum(field(BQ), axis=0, keepdims=True)
    c1 = step_0 / field(STEP)
    rest = 1.0 - c1
    norm_next = jnp.sum(
        c1 * c1 * field(VV) + 2.0 * c1 * rest * field(VB) + rest * rest * field(BB), axis=0, keepdims=True
    )
    turn = norm_next / norm_now
    c2 = rest + turn
    bend = jnp.sum(c1 * c1 * field(VU) + c1 * c2 * field(CROSS) + c2 * c2 * field(BQ), axis=0, keepdims=True)
    step_1 = norm_next / bend
    c1 = step_0 / own[0, :, STEP:STEP + 1]
    rest = 1.0 - c1
    c2 = rest + turn
    b, v = b_ref[...], v_ref[...]
    solution_ref[...] = step_0 * b + step_1 * (c1 * v + c2 * b)
    residual_ref[...] = c1 * v + rest * b - step_1 * (c1 * u_ref[...] + c2 * q_ref[...])


def everyone(block, axes):
    size = lax.axis_size(axes)
    copies = jnp.broadcast_to(block[None], (size, *block.shape))
    return lax.all_to_all(copies, axes, split_axis=0, concat_axis=0, tiled=True).reshape(-1, *block.shape[1:])


def col_order(size):
    return [0, *range(size - 1, 0, -1)]


def diagonals(size):
    return [shift for shift in range(size) if (shift >> 1).bit_count() > 1]


def row_order(size):
    far = diagonals(size)
    near = [1 << place for place in range(1, size.bit_length() - 1)]
    return far + near + [shift + 1 for shift in near] + [1]


def swap(block, shift, axis):
    size = lax.axis_size(axis)
    return lax.ppermute(block, axis, [(i, i ^ shift) for i in range(size)]) if shift else block


def shards(confidence, item_blocks, counts, item_factors):
    slots, width, _ = confidence.shape
    factor_width = item_factors.shape[1]
    groups = lax.axis_size("row")
    per_owner = slots // groups
    vmem = pl.BlockSpec(memory_space=pltpu.VMEM)
    smem = pl.BlockSpec(memory_space=pltpu.SMEM)

    params = pltpu.CompilerParams(vmem_limit_bytes=VMEM_LIMIT)

    def tiles(count):
        return jax.ShapeDtypeStruct((count, width, factor_width), item_factors.dtype)

    early = diagonals(groups)
    small = [jax.ShapeDtypeStruct(array.shape, array.dtype) for array in (item_blocks, counts, item_factors)]
    *loaded, blocks_here, counts_here, block_here = pl.pallas_call(
        load_kernel,
        out_shape=[tiles(per_owner if shift in early else 2 * per_owner) for shift in range(groups)] + small,
        in_specs=[pl.BlockSpec(memory_space=pl.ANY)] * 4,
        out_specs=[vmem] * (groups + 3),
        scratch_shapes=[pltpu.SemaphoreType.DMA((groups + 3,))],
        compiler_params=params,
    )(*[pltpu.with_memory_space_constraint(array, pltpu.HBM) for array in (confidence, item_blocks, counts, item_factors)])
    cols = lax.axis_size("col")
    blocks = [swap(item_factors, shift, "col") if shift else block_here for shift in col_order(cols)]
    weights = {shift: swap(loaded[shift], shift, "row") for shift in early}
    late = [shift for shift in range(groups) if shift not in early]
    parcels = pl.pallas_call(
        functools.partial(pick_kernel, groups, cols),
        out_shape=[tiles(per_owner if shift in early else 2 * per_owner) for shift in range(groups)],
        in_specs=[smem] * 2 + [vmem] * (cols + len(late)),
        out_specs=[vmem] * groups,
        input_output_aliases={2 + cols + place: shift for place, shift in enumerate(late)},
        scratch_shapes=[pltpu.VMEM((cols, width, factor_width), item_factors.dtype)],
        compiler_params=params,
    )(blocks_here, counts_here, *blocks, *[loaded[shift] for shift in late])
    items = {shift: swap(parcels[shift], shift, "row") for shift in [*row_order(groups), 0]}

    field = jax.ShapeDtypeStruct((width, factor_width), jnp.float32)
    b, q, v, u, stats = pl.pallas_call(
        krylov_kernel,
        out_shape=[field] * 4 + [jax.ShapeDtypeStruct((1, 1, factor_width), jnp.float32)],
        in_specs=[[vmem] * len(late), [[vmem] * 2] * len(early)],
        out_specs=[vmem] * 5,
        compiler_params=params,
    )([items[shift] for shift in items if shift in late], [[weights[shift], items[shift]] for shift in early])
    every = everyone(stats, ("row", "col"))
    return pl.pallas_call(
        finish_kernel,
        out_shape=[field] * 2,
        in_specs=[vmem] * 6,
        out_specs=[vmem] * 2,
        compiler_params=params,
    )(every, stats, b, q, v, u)


def solution(mesh):
    return jax.shard_map(
        shards,
        mesh=mesh,
        in_specs=(
            P(("row", "col"), None, None),
            P(("row", "col")),
            P(("row", "col")),
            P(("row", "col"), None),
        ),
        out_specs=(P(("row", "col"), None), P(("row", "col"), None)),
        check_vma=False,
    )
```

time: 194 us -> 37.7 us (0.19)
  blocking collectives: 182 us -> 10.3 us
  starting transfers between devices: 0 us -> 14.7 us
  waiting for transfers between devices: 0 us -> 7.6 us
  Pallas kernels: 0 us -> 4.25 us
  between operations: 4.72 us -> 0.68 us
  other arithmetic: 3.47 us -> 0 us
    psum x3 -> x0, blocking collectives: 119 us -> none  [the longest x2 80.4 us: squared_norm(): return lax.psum(jnp.sum(vector * vector), ('row', 'col'))]
    all_gather x3 -> x0, blocking collectives: 33.9 us -> none  [the longest x2 18.6 us: shards(): gathered = lax.all_gather(dirs_low, 'row', axis=0, tiled=True)]
    all_to_all x3 -> x1, blocking collectives: 29.4 us -> 10.3 us  [everyone(): lax.all_to_all(copies, axes, split_axis=0, concat_axis=0, tiled=True)]
    ppermute x0 -> x12, starting transfers between devices: none -> 14.7 us  [swap(): lax.ppermute(block, axis, [(i, i ^ shift) for i in range(size)])]
    ppermute x0 -> x12, waiting for transfers between devices: none -> 7.6 us  [swap(): lax.ppermute(block, axis, [(i, i ^ shift) for i in range(size)])]
    pallas_call x0 -> x4, Pallas kernels: none -> 4.25 us  [the longest x1 1.54 us: shards(): pl.pallas_call(krylov_kernel, out_shape=[field] * 4 + [jax.ShapeDtypeStru...]
    reduce_sum x6 -> x0, other arithmetic: 1.98 us -> none  [the longest x2 1.25 us: shards(): step_size = norm_now / lax.psum(jnp.sum(direction * image), ('row', 'col'))]
  transfers between devices with their start and end apart: 0 -> 12, of which waited for: 0 -> 6; matrix products, arithmetic and copies ran while one was open for 0% -> 0% of each run, Pallas kernels for 0% -> 5%
where the time goes in v1:
time: 37.7 us; the launch traced here: 37.5 us
  starting transfers between devices  14.7 us (39%)
  blocking collectives  10.3 us (27%)
  waiting for transfers between devices  7.6 us (20%)
  Pallas kernels  4.25 us (11%)
  between operations  0.68 us (2%)
    ppermute x12, starting transfers between devices, swap(): lax.ppermute(block, axis, [(i, i ^ shift) for i in range(size)])  14.7 us
    all_to_all x1, blocking collectives, everyone(): lax.all_to_all(copies, axes, split_axis=0, concat_axis=0, tiled=True)  10.3 us
    ppermute x12, waiting for transfers between devices, swap(): lax.ppermute(block, axis, [(i, i ^ shift) for i in range(size)])  7.6 us
    pallas_call x1, Pallas kernels, shards(): pl.pallas_call(krylov_kernel, out_shape=[field] * 4 + [jax.ShapeDtypeStru...  1.54 us
    pallas_call x1, Pallas kernels, shards(): pl.pallas_call(load_kernel, out_shape=[tiles(per_owner if shift in early...  1.16 us
    pallas_call x1, Pallas kernels, shards(): pl.pallas_call(finish_kernel, out_shape=[field] * 2, in_specs=[vmem] * 6,...  0.87 us
  transfers between devices with their start and end apart: 12, of which 6 were waited for; matrix products, arithmetic and copies ran while one was open for 0% of the time, Pallas kernels for 5%

profile of v1, /device:TPU:0, one launch (start us, length us, event | category | flops | bytes accessed | tf_op | source)
XLA Modules:
  0.0 37.5 jit_solution(9210499297614209538)
XLA Ops:
  0.6 5.1 %collective-permute-start = (bf16[128,128]{1,0:T(8,128)(2,1)}, bf16[128,128]{1,0:T(8,128)(2,1)S(1)}, u32[]{:S(2)}, u32[]{:S(2)}) collective-permute-start(bf16[128,128]{1,0:T(8,128)(2,1)} %block.1), channel_id=1, source_target_pairs={{0,3},{1,2},{2,1},{3,0},{4,7},{5,6},{6,5},{7,4},{8,11},{9,10},{10,... | collective-permute-start | bytes 98312 | tf_op jit(solution)/shard_map/ppermute | solution.py:146
  5.7 0.0 collective-permute-start.2
  5.7 0.6 %collective-permute-start.1 = (bf16[128,128]{1,0:T(8,128)(2,1)}, bf16[128,128]{1,0:T(8,128)(2,1)S(1)}, u32[]{:S(2)}, u32[]{:S(2)}) collective-permute-start(bf16[128,128]{1,0:T(8,128)(2,1)} %block.1), channel_id=1, source_target_pairs={{0,2},{1,3},{2,0},{3,1},{4,6},{5,7},{6,4},{7,5},{8,10},{9,11},{10,... | collective-permute-start | bytes 98312 | tf_op jit(solution)/shard_map/ppermute | solution.py:146
  6.4 1.2 %shard_map.59 = (bf16[4,128,128]{2,1,0:T(8,128)(2,1)S(1)}, bf16[4,128,128]{2,1,0:T(8,128)(2,1)S(1)}, bf16[4,128,128]{2,1,0:T(8,128)(2,1)S(1)}, bf16[4,128,128]{2...) custom-call(bf16[16,128,128]{2,1,0:T(8,128)(2,1)} %confidence.1, ...), custom_call_target="tpu_custom_call" | custom-call | tf_op jit(solution)/shard_map/pallas_call | solution.py:164
  7.6 2.7 %collective-permute-start.8 = (bf16[2,128,128]{2,1,0:T(8,128)(2,1)S(1)}, bf16[2,128,128]{2,1,0:T(8,128)(2,1)S(1)}, u32[]{:S(2)}, u32[]{:S(2)}) collective-permute-start(bf16[2,128,128]{2,1,0:T(8,128)(2,1)S(1)} %get-tuple-element.41), channel_id=1, source_target_pairs={{0,24},{4,28},{8,16},{12,20},{16,8},{20,12},{24,0},{28,4},{1,25},{... | collective-permute-start | bytes 196616 | tf_op jit(solution)/shard_map/ppermute | solution.py:146
  10.2 0.0 collective-permute-start.10
  10.2 0.0 collective-permute-done.refs_1_
  10.2 0.0 collective-permute-done.2.refs_3_
  10.2 0.7 %collective-permute-done.1.refs_2_ = bf16[128,128]{1,0:T(8,128)(2,1)S(1)} collective-permute-done((bf16[128,128]{1,0:T(8,128)(2,1)}, bf16[128,128]{1,0:T(8,128)(2,1)S(1)}, u32[]{:S(2)}, u32[]{:S(2)}) %collective-permute-start.1) | collective-permute-done | bytes 32800 | tf_op jit(solution)/shard_map/ppermute | solution.py:146
  10.9 0.7 %shard_map.60 = (bf16[4,128,128]{2,1,0:T(8,128)(2,1)S(1)}, bf16[4,128,128]{2,1,0:T(8,128)(2,1)S(1)}, bf16[4,128,128]{2,1,0:T(8,128)(2,1)S(1)}, bf16[4,128,128]{2...) custom-call(s32[16]{0:T(128)S(1)} %get-tuple-element.26.item_blocks,, ...), custom_call_target="tpu_custom_call", output_to_operand_aliasing={{0}: (6, {}), {1}: (7, {}), {2}: (8, {}), {3}: (9, {}), {4}... | custom-call | tf_op jit(solution)/shard_map/pallas_call | solution.py:176
  11.6 2.5 %collective-permute-start.9 = (bf16[2,128,128]{2,1,0:T(8,128)(2,1)S(1)}, bf16[2,128,128]{2,1,0:T(8,128)(2,1)S(1)}, u32[]{:S(2)}, u32[]{:S(2)}) collective-permute-start(bf16[2,128,128]{2,1,0:T(8,128)(2,1)S(1)} %get-tuple-element.42), channel_id=1, source_target_pairs={{0,24},{4,28},{8,16},{12,20},{16,8},{20,12},{24,0},{28,4},{1,25},{... | collective-permute-start | bytes 196616 | tf_op jit(solution)/shard_map/ppermute | solution.py:146
  14.1 0.0 collective-permute-start.11
  14.1 1.2 %collective-permute-start.3 = (bf16[4,128,128]{2,1,0:T(8,128)(2,1)S(1)}, bf16[4,128,128]{2,1,0:T(8,128)(2,1)S(1)}, u32[]{:S(2)}, u32[]{:S(2)}) collective-permute-start(bf16[4,128,128]{2,1,0:T(8,128)(2,1)S(1)} %get-tuple-element.35), channel_id=1, source_target_pairs={{0,8},{4,12},{8,0},{12,4},{16,24},{20,28},{24,16},{28,20},{1,9},{5... | collective-permute-start | bytes 393224 | tf_op jit(solution)/shard_map/ppermute | solution.py:146
  15.3 0.0 collective-permute-done.8.split_0__0_
  15.3 1.5 %collective-permute-start.4 = (bf16[4,128,128]{2,1,0:T(8,128)(2,1)S(1)}, bf16[4,128,128]{2,1,0:T(8,128)(2,1)S(1)}, u32[]{:S(2)}, u32[]{:S(2)}) collective-permute-start(bf16[4,128,128]{2,1,0:T(8,128)(2,1)S(1)} %get-tuple-element.36), channel_id=1, source_target_pairs={{0,16},{4,20},{8,24},{12,28},{16,0},{20,4},{24,8},{28,12},{1,17},{... | collective-permute-start | bytes 393224 | tf_op jit(solution)/shard_map/ppermute | solution.py:146
  16.9 0.0 collective-permute-done.10.split_1__0_
  16.9 0.4 %collective-permute-start.5 = (bf16[4,128,128]{2,1,0:T(8,128)(2,1)S(1)}, bf16[4,128,128]{2,1,0:T(8,128)(2,1)S(1)}, u32[]{:S(2)}, u32[]{:S(2)}) collective-permute-start(bf16[4,128,128]{2,1,0:T(8,128)(2,1)S(1)} %get-tuple-element.37), channel_id=1, source_target_pairs={{0,12},{4,8},{8,4},{12,0},{16,28},{20,24},{24,20},{28,16},{1,13},{... | collective-permute-start | bytes 393224 | tf_op jit(solution)/shard_map/ppermute | solution.py:146
  17.3 0.0 collective-permute-done.9.split_0__1_
  17.3 0.6 %collective-permute-start.6 = (bf16[4,128,128]{2,1,0:T(8,128)(2,1)S(1)}, bf16[4,128,128]{2,1,0:T(8,128)(2,1)S(1)}, u32[]{:S(2)}, u32[]{:S(2)}) collective-permute-start(bf16[4,128,128]{2,1,0:T(8,128)(2,1)S(1)} %get-tuple-element.38), channel_id=1, source_target_pairs={{0,20},{4,16},{8,28},{12,24},{16,4},{20,0},{24,12},{28,8},{1,21},{... | collective-permute-start | bytes 393224 | tf_op jit(solution)/shard_map/ppermute | solution.py:146
  17.9 1.5 %collective-permute-done.11.split_1__1_ = bf16[2,128,128]{2,1,0:T(8,128)(2,1)S(1)} collective-permute-done((bf16[2,128,128]{2,1,0:T(8,128)(2,1)S(1)}, bf16[2,128,128]{2,1,0:T(8,128)(2,1)S(1)}, u32[]{:S(2)}, u32[]{:S(2)}) %collective-permute-start.11) | collective-permute-done | bytes 65568 | tf_op jit(solution)/shard_map/ppermute | solution.py:146
  19.4 0.0 collective-permute-start.7
  19.4 1.6 %collective-permute-done.3.whole_0_ = bf16[4,128,128]{2,1,0:T(8,128)(2,1)S(1)} collective-permute-done((bf16[4,128,128]{2,1,0:T(8,128)(2,1)S(1)}, bf16[4,128,128]{2,1,0:T(8,128)(2,1)S(1)}, u32[]{:S(2)}, u32[]{:S(2)}) %collective-permute-start.3) | collective-permute-done | bytes 131104 | tf_op jit(solution)/shard_map/ppermute | solution.py:146
  20.9 1.1 %collective-permute-done.4.whole_1_ = bf16[4,128,128]{2,1,0:T(8,128)(2,1)S(1)} collective-permute-done((bf16[4,128,128]{2,1,0:T(8,128)(2,1)S(1)}, bf16[4,128,128]{2,1,0:T(8,128)(2,1)S(1)}, u32[]{:S(2)}, u32[]{:S(2)}) %collective-permute-start.4) | collective-permute-done | bytes 131104 | tf_op jit(solution)/shard_map/ppermute | solution.py:146
  22.1 1.8 %collective-permute-done.5.whole_2_ = bf16[4,128,128]{2,1,0:T(8,128)(2,1)S(1)} collective-permute-done((bf16[4,128,128]{2,1,0:T(8,128)(2,1)S(1)}, bf16[4,128,128]{2,1,0:T(8,128)(2,1)S(1)}, u32[]{:S(2)}, u32[]{:S(2)}) %collective-permute-start.5) | collective-permute-done | bytes 131104 | tf_op jit(solution)/shard_map/ppermute | solution.py:146
  23.9 0.9 %collective-permute-done.6.whole_3_ = bf16[4,128,128]{2,1,0:T(8,128)(2,1)S(1)} collective-permute-done((bf16[4,128,128]{2,1,0:T(8,128)(2,1)S(1)}, bf16[4,128,128]{2,1,0:T(8,128)(2,1)S(1)}, u32[]{:S(2)}, u32[]{:S(2)}) %collective-permute-start.6) | collective-permute-done | bytes 131104 | tf_op jit(solution)/shard_map/ppermute | solution.py:146
  24.8 0.0 collective-permute-done.7.whole_4_
  24.8 1.5 %shard_map.61 = (f32[128,128]{1,0:T(8,128)S(1)}, f32[128,128]{1,0:T(8,128)S(1)}, f32[128,128]{1,0:T(8,128)S(1)}, f32[128,128]{1,0:T(8,128)S(1)}, f32[1,1,128]{2,1,0:T(1,128)S(1)}) custom-call(bf16[4,128,128]{2,1,0:T(8,128)(2,1)S(1)} %collective-permute-done.3.whole_0_, bf16[4,128,128]{2,1,0:T(8,128)(2,1)S(1)} %collective-permute-done.4.whole_1_, ...), custom_call_target="tpu_custom_call" | custom-call | tf_op jit(solution)/shard_map/pallas_call | solution.py:188
  26.4 10.3 %all_to_all.5 = f32[32,1,1,128]{3,2,1,0:T(1,128)S(1)} all-to-all(f32[32,1,1,128]{3,2,1,0:T(1,128)S(1)} %broadcast_in_dim.9), channel_id=1, replica_groups=mesh['row'=8,'col'=4] {'row','col'}, dimensions={0} | all-to-all | bytes 32768 | tf_op jit(solution)/shard_map/all_to_all | solution.py:127
  36.6 0.9 %shard_map.62 = (f32[128,128]{1,0:T(8,128)}, f32[128,128]{1,0:T(8,128)}) custom-call(f32[32,1,128]{2,1,0:T(1,128)S(1)} %bitcast.2, f32[1,1,128]{2,1,0:T(1,128)S(1)} %get-tuple-element.45.own, f32[128,128]{1,0:T(8,128)S(1)} %get-tuple-element.46.b_ref, f32[128,128]{1,0:T(8,128)S(1)} %get-tuple-element.47.q_ref, f32[128,128]{1,0:T(8,128)S(1)} %get-tuple-element.48.v_ref, ...), custom_call_target="tpu_custom_call" | custom-call | tf_op jit(solution)/shard_map/pallas_call | solution.py:196
  (1 shorter events, 0.0 us)
Async XLA Ops:
  0.6 9.6 %collective-permute-start = (bf16[128,128]{1,0:T(8,128)(2,1)}, bf16[128,128]{1,0:T(8,128)(2,1)S(1)}, u32[]{:S(2)}, u32[]{:S(2)}) collective-permute-start(bf16[128,128]{1,0:T(8,128)(2,1)} %block.1), channel_id=1, source_target_pairs={{0,3},{1,2},{2,1},{3,0},{4,7},{5,6},{6,5},{7,4},{8,11},{9,10},{10,... | collective-permute-start | bytes 98312 | tf_op jit(solution)/shard_map/ppermute | solution.py:146
  5.7 4.5 %collective-permute-start.2 = (bf16[128,128]{1,0:T(8,128)(2,1)}, bf16[128,128]{1,0:T(8,128)(2,1)S(1)}, u32[]{:S(2)}, u32[]{:S(2)}) collective-permute-start(bf16[128,128]{1,0:T(8,128)(2,1)} %block.1), channel_id=1, source_target_pairs={{0,1},{1,0},{2,3},{3,2},{4,5},{5,4},{6,7},{7,6},{8,9},{9,8},{10,11... | collective-permute-start | bytes 98312 | tf_op jit(solution)/shard_map/ppermute | solution.py:146
  5.7 5.1 %collective-permute-start.1 = (bf16[128,128]{1,0:T(8,128)(2,1)}, bf16[128,128]{1,0:T(8,128)(2,1)S(1)}, u32[]{:S(2)}, u32[]{:S(2)}) collective-permute-start(bf16[128,128]{1,0:T(8,128)(2,1)} %block.1), channel_id=1, source_target_pairs={{0,2},{1,3},{2,0},{3,1},{4,6},{5,7},{6,4},{7,5},{8,10},{9,11},{10,... | collective-permute-start | bytes 98312 | tf_op jit(solution)/shard_map/ppermute | solution.py:146
  7.6 7.8 %collective-permute-start.8 = (bf16[2,128,128]{2,1,0:T(8,128)(2,1)S(1)}, bf16[2,128,128]{2,1,0:T(8,128)(2,1)S(1)}, u32[]{:S(2)}, u32[]{:S(2)}) collective-permute-start(bf16[2,128,128]{2,1,0:T(8,128)(2,1)S(1)} %get-tuple-element.41), channel_id=1, source_target_pairs={{0,24},{4,28},{8,16},{12,20},{16,8},{20,12},{24,0},{28,4},{1,25},{... | collective-permute-start | bytes 196616 | tf_op jit(solution)/shard_map/ppermute | solution.py:146
  10.2 6.6 %collective-permute-start.10 = (bf16[2,128,128]{2,1,0:T(8,128)(2,1)S(1)}, bf16[2,128,128]{2,1,0:T(8,128)(2,1)S(1)}, u32[]{:S(2)}, u32[]{:S(2)}) collective-permute-start(bf16[2,128,128]{2,1,0:T(8,128)(2,1)S(1)} %get-tuple-element.43), channel_id=1, source_target_pairs={{0,28},{4,24},{8,20},{12,16},{16,12},{20,8},{24,4},{28,0},{1,29},{... | collective-permute-start | bytes 196616 | tf_op jit(solution)/shard_map/ppermute | solution.py:146
  11.6 5.7 %collective-permute-start.9 = (bf16[2,128,128]{2,1,0:T(8,128)(2,1)S(1)}, bf16[2,128,128]{2,1,0:T(8,128)(2,1)S(1)}, u32[]{:S(2)}, u32[]{:S(2)}) collective-permute-start(bf16[2,128,128]{2,1,0:T(8,128)(2,1)S(1)} %get-tuple-element.42), channel_id=1, source_target_pairs={{0,24},{4,28},{8,16},{12,20},{16,8},{20,12},{24,0},{28,4},{1,25},{... | collective-permute-start | bytes 196616 | tf_op jit(solution)/shard_map/ppermute | solution.py:146
  14.1 5.3 %collective-permute-start.11 = (bf16[2,128,128]{2,1,0:T(8,128)(2,1)S(1)}, bf16[2,128,128]{2,1,0:T(8,128)(2,1)S(1)}, u32[]{:S(2)}, u32[]{:S(2)}) collective-permute-start(bf16[2,128,128]{2,1,0:T(8,128)(2,1)S(1)} %get-tuple-element.44), channel_id=1, source_target_pairs={{0,28},{4,24},{8,20},{12,16},{16,12},{20,8},{24,4},{28,0},{1,29},{... | collective-permute-start | bytes 196616 | tf_op jit(solution)/shard_map/ppermute | solution.py:146
  14.1 6.8 %collective-permute-start.3 = (bf16[4,128,128]{2,1,0:T(8,128)(2,1)S(1)}, bf16[4,128,128]{2,1,0:T(8,128)(2,1)S(1)}, u32[]{:S(2)}, u32[]{:S(2)}) collective-permute-start(bf16[4,128,128]{2,1,0:T(8,128)(2,1)S(1)} %get-tuple-element.35), channel_id=1, source_target_pairs={{0,8},{4,12},{8,0},{12,4},{16,24},{20,28},{24,16},{28,20},{1,9},{5... | collective-permute-start | bytes 393224 | tf_op jit(solution)/shard_map/ppermute | solution.py:146
  15.3 6.7 %collective-permute-start.4 = (bf16[4,128,128]{2,1,0:T(8,128)(2,1)S(1)}, bf16[4,128,128]{2,1,0:T(8,128)(2,1)S(1)}, u32[]{:S(2)}, u32[]{:S(2)}) collective-permute-start(bf16[4,128,128]{2,1,0:T(8,128)(2,1)S(1)} %get-tuple-element.36), channel_id=1, source_target_pairs={{0,16},{4,20},{8,24},{12,28},{16,0},{20,4},{24,8},{28,12},{1,17},{... | collective-permute-start | bytes 393224 | tf_op jit(solution)/shard_map/ppermute | solution.py:146
  16.9 7.0 %collective-permute-start.5 = (bf16[4,128,128]{2,1,0:T(8,128)(2,1)S(1)}, bf16[4,128,128]{2,1,0:T(8,128)(2,1)S(1)}, u32[]{:S(2)}, u32[]{:S(2)}) collective-permute-start(bf16[4,128,128]{2,1,0:T(8,128)(2,1)S(1)} %get-tuple-element.37), channel_id=1, source_target_pairs={{0,12},{4,8},{8,4},{12,0},{16,28},{20,24},{24,20},{28,16},{1,13},{... | collective-permute-start | bytes 393224 | tf_op jit(solution)/shard_map/ppermute | solution.py:146
  17.3 7.5 %collective-permute-start.6 = (bf16[4,128,128]{2,1,0:T(8,128)(2,1)S(1)}, bf16[4,128,128]{2,1,0:T(8,128)(2,1)S(1)}, u32[]{:S(2)}, u32[]{:S(2)}) collective-permute-start(bf16[4,128,128]{2,1,0:T(8,128)(2,1)S(1)} %get-tuple-element.38), channel_id=1, source_target_pairs={{0,20},{4,16},{8,28},{12,24},{16,4},{20,0},{24,12},{28,8},{1,21},{... | collective-permute-start | bytes 393224 | tf_op jit(solution)/shard_map/ppermute | solution.py:146
  19.4 5.4 %collective-permute-start.7 = (bf16[4,128,128]{2,1,0:T(8,128)(2,1)S(1)}, bf16[4,128,128]{2,1,0:T(8,128)(2,1)S(1)}, u32[]{:S(2)}, u32[]{:S(2)}) collective-permute-start(bf16[4,128,128]{2,1,0:T(8,128)(2,1)S(1)} %get-tuple-element.39), channel_id=1, source_target_pairs={{0,4},{4,0},{8,12},{12,8},{16,20},{20,16},{24,28},{28,24},{1,5},{5... | collective-permute-start | bytes 393224 | tf_op jit(solution)/shard_map/ppermute | solution.py:146

commit v2 on v1

v2 whole, which is shorter than its diff:
```python
import functools

import jax
import jax.numpy as jnp
from jax import lax
from jax.experimental import pallas as pl
from jax.experimental.pallas import tpu as pltpu
from jax.sharding import PartitionSpec as P

ridge = 2.0
PICK_FLOPS = 20_000_000_000
VMEM_LIMIT = 48 * 1024 * 1024
BB, BQ, VV, VB, VU, CROSS, STEP = range(7)


def dot(a, b, contract):
    return lax.dot_general(a, b, ((contract[:1], contract[1:]), ((), ())), preferred_element_type=jnp.float32)


def total(a):
    return jnp.sum(a, axis=(0, 1), keepdims=True)


def load_kernel(groups, confidence, item_blocks, counts, block, far, *refs):
    parcels, (marks, block_here, blocks_here, counts_here, arrived) = refs[:-5], refs[-5:]
    per_owner = confidence.shape[0] // groups
    cols = marks.shape[1]
    row, col = lax.axis_index("row"), lax.axis_index("col")
    pairs = [(item_blocks, blocks_here), (counts, counts_here)]
    targets = [(groups - 2, far, 0), (groups - 1, far, per_owner)]
    targets += [(shift, parcel, 0) for shift, parcel in enumerate(parcels)]
    pairs += [
        (confidence.at[pl.ds((row ^ shift) * per_owner, per_owner)], target.at[pl.ds(first, per_owner)])
        for shift, target, first in targets
    ]
    pairs.append((block, block_here))
    copies = [pltpu.make_async_copy(source, target, arrived.at[i]) for i, (source, target) in enumerate(pairs)]
    for copy in copies:
        copy.start()
    for copy in copies[:2]:
        copy.wait()
    shift_col = lax.broadcasted_iota(jnp.int32, marks.shape[1:], 0)
    for shift in range(groups):
        owner = row ^ shift
        for place in range(per_owner):
            chosen = jnp.where(place < counts_here[owner], blocks_here[owner * per_owner + place] ^ col, cols)

            marks[shift * per_owner + place] = jnp.where(shift_col == chosen, 1.0, 0.0).astype(marks.dtype)
    for copy in copies[2:]:
        copy.wait()


def pick_kernel(groups, cols, late, marks, *refs):
    blocks, (far, sibling, *parcels, slab) = refs[:cols], refs[cols + len(late):]
    for shift, block in zip(col_order(cols), blocks):
        slab[shift] = block[...]
    per_owner = marks.shape[0] // groups
    rows = marks.shape[2]
    targets = [(groups - 2, far, 0), (groups - 1, far, per_owner), (1, sibling, 0)]
    targets += [(shift, parcel, per_owner) for shift, parcel in zip(late, parcels)]
    for shift, target, first in targets:
        for place in range(per_owner):

            def add(shift_col, tile, slot=shift * per_owner + place):
                return tile + slab[shift_col].reshape(-1, *marks.shape[2:]) * marks[slot, shift_col][None]

            tile = jnp.zeros((slab.shape[1] // rows, *marks.shape[2:]), slab.dtype)
            tile = lax.fori_loop(0, cols, add, tile, unroll=cols <= 4)
            target[first + place] = tile.reshape(slab.shape[1:])


def tiles_of(far, sibling, whole):
    for weights, items in (far, sibling):
        part = weights.shape[0] // 2
        yield joined(weights[:part], items[:part])
    yield joined(sibling[0][part:], sibling[1][part:])
    for parcel in whole:
        yield joined(parcel[:part], parcel[part:])


def joined(weights, items):
    w = jnp.concatenate([weights[place] for place in range(weights.shape[0])], axis=1)
    return items.reshape(-1, items.shape[-1]), w


def apply(parts, field):
    low = field.astype(jnp.bfloat16)
    image = ridge * field
    energy = 0.0
    for x, w in tiles_of(*parts):
        scores = dot(low, x, (1, 1))
        weighted = w.astype(jnp.float32) * scores
        energy = energy + weighted * scores
        image = image + dot(weighted.astype(jnp.bfloat16), x, (1, 0))
    squares = total(field * field)
    return image, squares, ridge * squares + total(energy)


def krylov_kernel(far_items, whole, far_weights, sibling, b_ref, q_ref, v_ref, u_ref, stats):
    parts = (far_weights, far_items), sibling, whole
    b = jnp.zeros(b_ref.shape, jnp.float32)
    for x, w in tiles_of(*parts):
        b = b + dot(w, x, (1, 0))
    q, bb, bq = apply(parts, b)
    step = jnp.where(bq > 0, bb / bq, 1.0)
    v = b - step * q
    u, vv, vu = apply(parts, v)
    b_ref[...] = b
    q_ref[...] = q
    v_ref[...] = v
    u_ref[...] = u
    values = {BB: bb, BQ: bq, VV: vv, VB: total(v * b), VU: vu, CROSS: 2.0 * total(v * q), STEP: step}
    lane = lax.broadcasted_iota(jnp.int32, stats.shape[1:], 1)
    packed = jnp.zeros(stats.shape[1:], jnp.float32)
    for place, value in values.items():
        packed = jnp.where(lane == place, value, packed)
    stats[0] = packed


def finish_kernel(every, own, b_ref, q_ref, v_ref, u_ref, solution_ref, residual_ref):
    def field(place):
        return every[:, 0, place:place + 1]

    norm_now = jnp.sum(field(BB), axis=0, keepdims=True)
    step_0 = norm_now / jnp.sum(field(BQ), axis=0, keepdims=True)
    c1 = step_0 / field(STEP)
    rest = 1.0 - c1
    norm_next = jnp.sum(
        c1 * c1 * field(VV) + 2.0 * c1 * rest * field(VB) + rest * rest * field(BB), axis=0, keepdims=True
    )
    turn = norm_next / norm_now
    c2 = rest + turn
    bend = jnp.sum(c1 * c1 * field(VU) + c1 * c2 * field(CROSS) + c2 * c2 * field(BQ), axis=0, keepdims=True)
    step_1 = norm_next / bend
    c1 = step_0 / own[0, :, STEP:STEP + 1]
    rest = 1.0 - c1
    c2 = rest + turn
    b, v = b_ref[...], v_ref[...]
    solution_ref[...] = step_0 * b + step_1 * (c1 * v + c2 * b)
    residual_ref[...] = c1 * v + rest * b - step_1 * (c1 * u_ref[...] + c2 * q_ref[...])


def everyone(block, axes):
    size = lax.axis_size(axes)
    copies = jnp.broadcast_to(block[None], (size, *block.shape))
    return lax.all_to_all(copies, axes, split_axis=0, concat_axis=0, tiled=True).reshape(-1, *block.shape[1:])


def col_order(size):
    return [0, *sorted(range(1, size), key=lambda shift: shift != size >> 1)]


def row_order(size):
    near = [1 << place for place in range(1, size.bit_length() - 1)]
    near += [shift + 1 for shift in near]
    return [shift for shift in range(2, size - 2) if shift not in near] + near


def swap(block, shift, axis):
    size = lax.axis_size(axis)
    return lax.ppermute(block, axis, [(i, i ^ shift) for i in range(size)]) if shift else block


def shards(confidence, item_blocks, counts, item_factors):
    slots, width, _ = confidence.shape
    factor_width = item_factors.shape[1]
    groups = lax.axis_size("row")
    per_owner = slots // groups
    vmem = pl.BlockSpec(memory_space=pltpu.VMEM)

    params = pltpu.CompilerParams(vmem_limit_bytes=VMEM_LIMIT)

    def tiles(count):
        return jax.ShapeDtypeStruct((count, width, factor_width), item_factors.dtype)

    far = groups - 2
    cols = lax.axis_size("col")
    early, *loaded, marks, block_here = pl.pallas_call(
        functools.partial(load_kernel, groups),
        out_shape=[tiles(2 * per_owner if shift != 1 else per_owner) for shift in [far, *range(far)]]
        + [
            jax.ShapeDtypeStruct((slots, cols, 16, factor_width), item_factors.dtype),
            jax.ShapeDtypeStruct(item_factors.shape, item_factors.dtype),
        ],
        in_specs=[pl.BlockSpec(memory_space=pl.ANY)] * 4,
        out_specs=[vmem] * (far + 3),
        scratch_shapes=[
            pltpu.SMEM(item_blocks.shape, item_blocks.dtype),
            pltpu.SMEM(counts.shape, counts.dtype),
            pltpu.SemaphoreType.DMA((groups + 3,)),
        ],
        compiler_params=params,
    )(*[pltpu.with_memory_space_constraint(array, pltpu.HBM) for array in (confidence, item_blocks, counts, item_factors)])
    blocks = [swap(item_factors, shift, "col") if shift else block_here for shift in col_order(cols)]
    early = swap(early, far, "row")
    late = [0, *row_order(groups)]
    far_items, sibling_items, *parcels = pl.pallas_call(
        functools.partial(pick_kernel, groups, cols, late),
        out_shape=[tiles(2 * per_owner), tiles(per_owner)] + [tiles(2 * per_owner)] * len(late),
        in_specs=[vmem] * (1 + cols + len(late)),
        out_specs=[vmem] * (2 + len(late)),
        input_output_aliases={1 + cols + place: 2 + place for place in range(len(late))},
        scratch_shapes=[pltpu.VMEM((cols, width, factor_width), item_factors.dtype)],
        cost_estimate=pl.CostEstimate(flops=PICK_FLOPS, bytes_accessed=0, transcendentals=0),
        compiler_params=params,
    )(marks, *blocks, *[loaded[shift] for shift in late])
    far_items = swap(far_items, far, "row")
    whole = [swap(parcel, shift, "row") for shift, parcel in zip(late, parcels)]
    sibling = [
        swap(jnp.concatenate([own, passed[per_owner:]]), 1, "row")
        for own, passed in ((loaded[1], early), (sibling_items, far_items))
    ]

    field = jax.ShapeDtypeStruct((width, factor_width), jnp.float32)
    b, q, v, u, stats = pl.pallas_call(
        krylov_kernel,
        out_shape=[field] * 4 + [jax.ShapeDtypeStruct((1, 1, factor_width), jnp.float32)],
        in_specs=[vmem, [vmem] * len(whole), vmem, [vmem] * 2],
        out_specs=[vmem] * 5,
        compiler_params=params,
    )(far_items, whole, early, sibling)
    every = everyone(stats, ("row", "col"))
    return pl.pallas_call(
        finish_kernel,
        out_shape=[field] * 2,
        in_specs=[vmem] * 6,
        out_specs=[vmem] * 2,
        compiler_params=params,
    )(every, stats, b, q, v, u)


def solution(mesh):
    return jax.shard_map(
        shards,
        mesh=mesh,
        in_specs=(
            P(("row", "col"), None, None),
            P(("row", "col")),
            P(("row", "col")),
            P(("row", "col"), None),
        ),
        out_specs=(P(("row", "col"), None), P(("row", "col"), None)),
        check_vma=False,
    )
```

time: 37.7 us -> 35.9 us (0.952)
  waiting for transfers between devices: 7.6 us -> 5.16 us
  blocking collectives: 10.3 us -> 11.7 us
  Pallas kernels: 4.25 us -> 3.68 us
    ppermute x12 -> x11, waiting for transfers between devices: 7.6 us -> 5.16 us  [swap(): lax.ppermute(block, axis, [(i, i ^ shift) for i in range(size)])]
    all_to_all x1, blocking collectives: 10.3 us -> 11.7 us  [everyone(): lax.all_to_all(copies, axes, split_axis=0, concat_axis=0, tiled=True)]
    ppermute x12 -> x11, starting transfers between devices: 14.7 us -> 14.5 us  [swap(): lax.ppermute(block, axis, [(i, i ^ shift) for i in range(size)])]
  transfers between devices with their start and end apart: 12 -> 11, of which waited for: 6 -> 6; matrix products, arithmetic and copies ran while one was open for 0% -> 0% of each run, Pallas kernels for 5% -> 4%
where the time goes in v2:
time: 35.9 us; the launch traced here: 35.7 us
  starting transfers between devices  14.5 us (40%)
  blocking collectives  11.7 us (33%)
  waiting for transfers between devices  5.16 us (14%)
  Pallas kernels  3.68 us (10%)
  between operations  0.69 us (2%)
    ppermute x11, starting transfers between devices, swap(): lax.ppermute(block, axis, [(i, i ^ shift) for i in range(size)])  14.5 us
    all_to_all x1, blocking collectives, everyone(): lax.all_to_all(copies, axes, split_axis=0, concat_axis=0, tiled=True)  11.7 us
    ppermute x11, waiting for transfers between devices, swap(): lax.ppermute(block, axis, [(i, i ^ shift) for i in range(size)])  5.16 us
    pallas_call x1, Pallas kernels, shards(): pl.pallas_call(krylov_kernel, out_shape=[field] * 4 + [jax.ShapeDtypeStru...  1.32 us
    pallas_call x1, Pallas kernels, shards(): pl.pallas_call(functools.partial(load_kernel, groups), out_shape=[tiles(2...  1.16 us
    pallas_call x1, Pallas kernels, shards(): pl.pallas_call(finish_kernel, out_shape=[field] * 2, in_specs=[vmem] * 6,...  0.87 us
  transfers between devices with their start and end apart: 11, of which 6 were waited for; matrix products, arithmetic and copies ran while one was open for 0% of the time, Pallas kernels for 4%

profile of v2, /device:TPU:0, one launch (start us, length us, event | category | flops | bytes accessed | tf_op | source)
XLA Modules:
  0.0 35.7 jit_solution(7942101393156642521)
XLA Ops:
  0.6 4.1 %collective-permute-start = (bf16[128,128]{1,0:T(8,128)(2,1)}, bf16[128,128]{1,0:T(8,128)(2,1)S(1)}, u32[]{:S(2)}, u32[]{:S(2)}) collective-permute-start(bf16[128,128]{1,0:T(8,128)(2,1)} %block.1), channel_id=1, source_target_pairs={{0,2},{1,3},{2,0},{3,1},{4,6},{5,7},{6,4},{7,5},{8,10},{9,11},{10,... | collective-permute-start | bytes 98312 | tf_op jit(solution)/shard_map/ppermute | solution.py:161
  4.7 1.3 %collective-permute-start.2 = (bf16[128,128]{1,0:T(8,128)(2,1)}, bf16[128,128]{1,0:T(8,128)(2,1)S(1)}, u32[]{:S(2)}, u32[]{:S(2)}) collective-permute-start(bf16[128,128]{1,0:T(8,128)(2,1)} %block.1), channel_id=1, source_target_pairs={{0,3},{1,2},{2,1},{3,0},{4,7},{5,6},{6,5},{7,4},{8,11},{9,10},{10,... | collective-permute-start | bytes 98312 | tf_op jit(solution)/shard_map/ppermute | solution.py:161
  6.1 0.2 collective-permute-start.1
  6.3 1.2 %shard_map.59 = (bf16[4,128,128]{2,1,0:T(8,128)(2,1)S(1)}, bf16[4,128,128]{2,1,0:T(8,128)(2,1)S(1)}, bf16[2,128,128]{2,1,0:T(8,128)(2,1)S(1)}, bf16[4,128,128]{2...) custom-call(bf16[16,128,128]{2,1,0:T(8,128)(2,1)} %confidence.1, ...), custom_call_target="tpu_custom_call" | custom-call | tf_op jit(solution)/shard_map/pallas_call | solution.py:178
  7.5 2.5 %collective-permute-start.8 = (bf16[4,128,128]{2,1,0:T(8,128)(2,1)S(1)}, bf16[4,128,128]{2,1,0:T(8,128)(2,1)S(1)}, u32[]{:S(2)}, u32[]{:S(2)}) collective-permute-start(bf16[4,128,128]{2,1,0:T(8,128)(2,1)S(1)} %get-tuple-element.36), channel_id=1, source_target_pairs={{0,24},{4,28},{8,16},{12,20},{16,8},{20,12},{24,0},{28,4},{1,25},{... | collective-permute-start | bytes 393224 | tf_op jit(solution)/shard_map/ppermute | solution.py:161
  10.0 0.0 collective-permute-done.refs_1_
  10.0 0.7 %collective-permute-done.2.refs_3_ = bf16[128,128]{1,0:T(8,128)(2,1)S(1)} collective-permute-done((bf16[128,128]{1,0:T(8,128)(2,1)}, bf16[128,128]{1,0:T(8,128)(2,1)S(1)}, u32[]{:S(2)}, u32[]{:S(2)}) %collective-permute-start.2) | collective-permute-done | bytes 32800 | tf_op jit(solution)/shard_map/ppermute | solution.py:161
  10.7 0.0 collective-permute-done.1.refs_2_
  10.7 0.3 shard_map.60
  11.0 2.5 %collective-permute-start.3 = (bf16[4,128,128]{2,1,0:T(8,128)(2,1)S(1)}, bf16[4,128,128]{2,1,0:T(8,128)(2,1)S(1)}, u32[]{:S(2)}, u32[]{:S(2)}) collective-permute-start(bf16[4,128,128]{2,1,0:T(8,128)(2,1)S(1)} %get-tuple-element.30), channel_id=1, source_target_pairs={{0,24},{4,28},{8,16},{12,20},{16,8},{20,12},{24,0},{28,4},{1,25},{... | collective-permute-start | bytes 393224 | tf_op jit(solution)/shard_map/ppermute | solution.py:161
  13.5 0.5 %collective-permute-start.4 = (bf16[4,128,128]{2,1,0:T(8,128)(2,1)S(1)}, bf16[4,128,128]{2,1,0:T(8,128)(2,1)S(1)}, u32[]{:S(2)}, u32[]{:S(2)}) collective-permute-start(bf16[4,128,128]{2,1,0:T(8,128)(2,1)S(1)} %get-tuple-element.32), channel_id=1, source_target_pairs={{0,8},{4,12},{8,0},{12,4},{16,24},{20,28},{24,16},{28,20},{1,9},{5... | collective-permute-start | bytes 393224 | tf_op jit(solution)/shard_map/ppermute | solution.py:161
  14.0 0.5 %collective-permute-start.5 = (bf16[4,128,128]{2,1,0:T(8,128)(2,1)S(1)}, bf16[4,128,128]{2,1,0:T(8,128)(2,1)S(1)}, u32[]{:S(2)}, u32[]{:S(2)}) collective-permute-start(bf16[4,128,128]{2,1,0:T(8,128)(2,1)S(1)} %get-tuple-element.33), channel_id=1, source_target_pairs={{0,16},{4,20},{8,24},{12,28},{16,0},{20,4},{24,8},{28,12},{1,17},{... | collective-permute-start | bytes 393224 | tf_op jit(solution)/shard_map/ppermute | solution.py:161
  14.5 0.0 collective-permute-start.6
  14.6 0.0 collective-permute-done.8.far_weights
  14.6 2.7 %collective-permute-start.7 = (bf16[4,128,128]{2,1,0:T(8,128)(2,1)S(1)}, bf16[4,128,128]{2,1,0:T(8,128)(2,1)S(1)}, u32[]{:S(2)}, u32[]{:S(2)}) collective-permute-start(bf16[4,128,128]{2,1,0:T(8,128)(2,1)S(1)} %get-tuple-element.35), channel_id=1, source_target_pairs={{0,20},{4,16},{8,28},{12,24},{16,4},{20,0},{24,12},{28,8},{1,21},{... | collective-permute-start | bytes 393224 | tf_op jit(solution)/shard_map/ppermute | solution.py:161
  17.3 0.3 collective-permute-done.3.far_items
  17.6 0.0 collective-permute-start.9
  17.7 2.8 %collective-permute-done.4.whole_1_ = bf16[4,128,128]{2,1,0:T(8,128)(2,1)S(1)} collective-permute-done((bf16[4,128,128]{2,1,0:T(8,128)(2,1)S(1)}, bf16[4,128,128]{2,1,0:T(8,128)(2,1)S(1)}, u32[]{:S(2)}, u32[]{:S(2)}) %collective-permute-start.4) | collective-permute-done | bytes 131104 | tf_op jit(solution)/shard_map/ppermute | solution.py:161
  20.5 0.0 collective-permute-start.10
  20.5 0.0 collective-permute-done.5.whole_2_
  20.5 0.4 %collective-permute-done.6.whole_3_ = bf16[4,128,128]{2,1,0:T(8,128)(2,1)S(1)} collective-permute-done((bf16[4,128,128]{2,1,0:T(8,128)(2,1)S(1)}, bf16[4,128,128]{2,1,0:T(8,128)(2,1)S(1)}, u32[]{:S(2)}, u32[]{:S(2)}) %collective-permute-start.6) | collective-permute-done | bytes 131104 | tf_op jit(solution)/shard_map/ppermute | solution.py:161
  20.9 0.4 %collective-permute-done.7.whole_4_ = bf16[4,128,128]{2,1,0:T(8,128)(2,1)S(1)} collective-permute-done((bf16[4,128,128]{2,1,0:T(8,128)(2,1)S(1)}, bf16[4,128,128]{2,1,0:T(8,128)(2,1)S(1)}, u32[]{:S(2)}, u32[]{:S(2)}) %collective-permute-start.7) | collective-permute-done | bytes 131104 | tf_op jit(solution)/shard_map/ppermute | solution.py:161
  21.3 0.0 collective-permute-done.9.sibling_0_
  21.3 0.5 %collective-permute-done.10.sibling_1_ = bf16[4,128,128]{2,1,0:T(8,128)(2,1)S(1)} collective-permute-done((bf16[4,128,128]{2,1,0:T(8,128)(2,1)S(1)}, bf16[4,128,128]{2,1,0:T(8,128)(2,1)S(1)}, u32[]{:S(2)}, u32[]{:S(2)}) %collective-permute-start.10) | collective-permute-done | bytes 131104 | tf_op jit(solution)/shard_map/ppermute | solution.py:161
  21.8 1.3 %shard_map.61 = (f32[128,128]{1,0:T(8,128)S(1)}, f32[128,128]{1,0:T(8,128)S(1)}, f32[128,128]{1,0:T(8,128)S(1)}, f32[128,128]{1,0:T(8,128)S(1)}, f32[1,1,128]{2,1,0:T(1,128)S(1)}) custom-call(bf16[4,128,128]{2,1,0:T(8,128)(2,1)S(1)} %collective-permute-done.3.far_items, bf16[4,128,128]{2,1,0:T(8,128)(2,1)S(1)} %get-tuple-element.31.whole_0_, ...), custom_call_target="tpu_custom_call" | custom-call | tf_op jit(solution)/shard_map/pallas_call | solution.py:215
  23.2 11.7 %all_to_all.5 = f32[32,1,1,128]{3,2,1,0:T(1,128)S(1)} all-to-all(f32[32,1,1,128]{3,2,1,0:T(1,128)S(1)} %broadcast_in_dim.9), channel_id=1, replica_groups=mesh['row'=8,'col'=4] {'row','col'}, dimensions={0} | all-to-all | bytes 32768 | tf_op jit(solution)/shard_map/all_to_all | solution.py:146
  34.9 0.9 %shard_map.62 = (f32[128,128]{1,0:T(8,128)}, f32[128,128]{1,0:T(8,128)}) custom-call(f32[32,1,128]{2,1,0:T(1,128)S(1)} %bitcast.2, f32[1,1,128]{2,1,0:T(1,128)S(1)} %get-tuple-element.39.own, f32[128,128]{1,0:T(8,128)S(1)} %get-tuple-element.40.b_ref, f32[128,128]{1,0:T(8,128)S(1)} %get-tuple-element.41.q_ref, f32[128,128]{1,0:T(8,128)S(1)} %get-tuple-element.42.v_ref, ...), custom_call_target="tpu_custom_call" | custom-call | tf_op jit(solution)/shard_map/pallas_call | solution.py:223
  (5 shorter events, 0.0 us)
Async XLA Ops:
  0.6 9.4 %collective-permute-start = (bf16[128,128]{1,0:T(8,128)(2,1)}, bf16[128,128]{1,0:T(8,128)(2,1)S(1)}, u32[]{:S(2)}, u32[]{:S(2)}) collective-permute-start(bf16[128,128]{1,0:T(8,128)(2,1)} %block.1), channel_id=1, source_target_pairs={{0,2},{1,3},{2,0},{3,1},{4,6},{5,7},{6,4},{7,5},{8,10},{9,11},{10,... | collective-permute-start | bytes 98312 | tf_op jit(solution)/shard_map/ppermute | solution.py:161
  4.7 5.9 %collective-permute-start.2 = (bf16[128,128]{1,0:T(8,128)(2,1)}, bf16[128,128]{1,0:T(8,128)(2,1)S(1)}, u32[]{:S(2)}, u32[]{:S(2)}) collective-permute-start(bf16[128,128]{1,0:T(8,128)(2,1)} %block.1), channel_id=1, source_target_pairs={{0,3},{1,2},{2,1},{3,0},{4,7},{5,6},{6,5},{7,4},{8,11},{9,10},{10,... | collective-permute-start | bytes 98312 | tf_op jit(solution)/shard_map/ppermute | solution.py:161
  6.1 4.6 %collective-permute-start.1 = (bf16[128,128]{1,0:T(8,128)(2,1)}, bf16[128,128]{1,0:T(8,128)(2,1)S(1)}, u32[]{:S(2)}, u32[]{:S(2)}) collective-permute-start(bf16[128,128]{1,0:T(8,128)(2,1)} %block.1), channel_id=1, source_target_pairs={{0,1},{1,0},{2,3},{3,2},{4,5},{5,4},{6,7},{7,6},{8,9},{9,8},{10,11... | collective-permute-start | bytes 98312 | tf_op jit(solution)/shard_map/ppermute | solution.py:161
  7.5 7.1 %collective-permute-start.8 = (bf16[4,128,128]{2,1,0:T(8,128)(2,1)S(1)}, bf16[4,128,128]{2,1,0:T(8,128)(2,1)S(1)}, u32[]{:S(2)}, u32[]{:S(2)}) collective-permute-start(bf16[4,128,128]{2,1,0:T(8,128)(2,1)S(1)} %get-tuple-element.36), channel_id=1, source_target_pairs={{0,24},{4,28},{8,16},{12,20},{16,8},{20,12},{24,0},{28,4},{1,25},{... | collective-permute-start | bytes 393224 | tf_op jit(solution)/shard_map/ppermute | solution.py:161
  11.0 6.6 %collective-permute-start.3 = (bf16[4,128,128]{2,1,0:T(8,128)(2,1)S(1)}, bf16[4,128,128]{2,1,0:T(8,128)(2,1)S(1)}, u32[]{:S(2)}, u32[]{:S(2)}) collective-permute-start(bf16[4,128,128]{2,1,0:T(8,128)(2,1)S(1)} %get-tuple-element.30), channel_id=1, source_target_pairs={{0,24},{4,28},{8,16},{12,20},{16,8},{20,12},{24,0},{28,4},{1,25},{... | collective-permute-start | bytes 393224 | tf_op jit(solution)/shard_map/ppermute | solution.py:161
  13.5 7.0 %collective-permute-start.4 = (bf16[4,128,128]{2,1,0:T(8,128)(2,1)S(1)}, bf16[4,128,128]{2,1,0:T(8,128)(2,1)S(1)}, u32[]{:S(2)}, u32[]{:S(2)}) collective-permute-start(bf16[4,128,128]{2,1,0:T(8,128)(2,1)S(1)} %get-tuple-element.32), channel_id=1, source_target_pairs={{0,8},{4,12},{8,0},{12,4},{16,24},{20,28},{24,16},{28,20},{1,9},{5... | collective-permute-start | bytes 393224 | tf_op jit(solution)/shard_map/ppermute | solution.py:161
  14.0 6.5 %collective-permute-start.5 = (bf16[4,128,128]{2,1,0:T(8,128)(2,1)S(1)}, bf16[4,128,128]{2,1,0:T(8,128)(2,1)S(1)}, u32[]{:S(2)}, u32[]{:S(2)}) collective-permute-start(bf16[4,128,128]{2,1,0:T(8,128)(2,1)S(1)} %get-tuple-element.33), channel_id=1, source_target_pairs={{0,16},{4,20},{8,24},{12,28},{16,0},{20,4},{24,8},{28,12},{1,17},{... | collective-permute-start | bytes 393224 | tf_op jit(solution)/shard_map/ppermute | solution.py:161
  14.5 6.4 %collective-permute-start.6 = (bf16[4,128,128]{2,1,0:T(8,128)(2,1)S(1)}, bf16[4,128,128]{2,1,0:T(8,128)(2,1)S(1)}, u32[]{:S(2)}, u32[]{:S(2)}) collective-permute-start(bf16[4,128,128]{2,1,0:T(8,128)(2,1)S(1)} %get-tuple-element.34), channel_id=1, source_target_pairs={{0,12},{4,8},{8,4},{12,0},{16,28},{20,24},{24,20},{28,16},{1,13},{... | collective-permute-start | bytes 393224 | tf_op jit(solution)/shard_map/ppermute | solution.py:161
  14.6 6.8 %collective-permute-start.7 = (bf16[4,128,128]{2,1,0:T(8,128)(2,1)S(1)}, bf16[4,128,128]{2,1,0:T(8,128)(2,1)S(1)}, u32[]{:S(2)}, u32[]{:S(2)}) collective-permute-start(bf16[4,128,128]{2,1,0:T(8,128)(2,1)S(1)} %get-tuple-element.35), channel_id=1, source_target_pairs={{0,20},{4,16},{8,28},{12,24},{16,4},{20,0},{24,12},{28,8},{1,21},{... | collective-permute-start | bytes 393224 | tf_op jit(solution)/shard_map/ppermute | solution.py:161
  17.6 3.7 %collective-permute-start.9 = (bf16[4,128,128]{2,1,0:T(8,128)(2,1)S(1)}, bf16[4,128,128]{2,1,0:T(8,128)(2,1)S(1)}, u32[]{:S(2)}, u32[]{:S(2)}) collective-permute-start(bf16[4,128,128]{2,1,0:T(8,128)(2,1)S(1)} %pad_maximum_fusion), channel_id=1, source_target_pairs={{0,4},{4,0},{8,12},{12,8},{16,20},{20,16},{24,28},{28,24},{1,5},{5... | collective-permute-start | bytes 393224 | tf_op jit(solution)/shard_map/ppermute | solution.py:161
  20.5 1.3 %collective-permute-start.10 = (bf16[4,128,128]{2,1,0:T(8,128)(2,1)S(1)}, bf16[4,128,128]{2,1,0:T(8,128)(2,1)S(1)}, u32[]{:S(2)}, u32[]{:S(2)}) collective-permute-start(bf16[4,128,128]{2,1,0:T(8,128)(2,1)S(1)} %pad_maximum_fusion.1), channel_id=1, source_target_pairs={{0,4},{4,0},{8,12},{12,8},{16,20},{20,16},{24,28},{28,24},{1,5},{5... | collective-permute-start | bytes 393224 | tf_op jit(solution)/shard_map/ppermute | solution.py:161

commit v3 on v2

--- a/solution.py
+++ b/solution.py
@@ -152,7 +152,7 @@
 
 def row_order(size):
     near = [1 << place for place in range(1, size.bit_length() - 1)]
-    near += [shift + 1 for shift in near]
+    near += [shift + 1 for shift in near[::-1]]
     return [shift for shift in range(2, size - 2) if shift not in near] + near
 
 

time: 35.9 us -> 35.9 us (level)
  waiting for transfers between devices: 5.16 us -> 4.73 us
  blocking collectives: 11.7 us -> 12.1 us
    all_to_all x1, blocking collectives: 11.7 us -> 12.1 us  [everyone(): lax.all_to_all(copies, axes, split_axis=0, concat_axis=0, tiled=True)]
    ppermute x11, waiting for transfers between devices: 5.16 us -> 4.73 us  [swap(): lax.ppermute(block, axis, [(i, i ^ shift) for i in range(size)])]
where the time goes in v3:
time: 35.9 us; the launch traced here: 35.7 us
  starting transfers between devices  14.5 us (40%)
  blocking collectives  12.1 us (34%)
  waiting for transfers between devices  4.73 us (13%)
  Pallas kernels  3.68 us (10%)
  between operations  0.69 us (2%)
    ppermute x11, starting transfers between devices, swap(): lax.ppermute(block, axis, [(i, i ^ shift) for i in range(size)])  14.5 us
    all_to_all x1, blocking collectives, everyone(): lax.all_to_all(copies, axes, split_axis=0, concat_axis=0, tiled=True)  12.1 us
    ppermute x11, waiting for transfers between devices, swap(): lax.ppermute(block, axis, [(i, i ^ shift) for i in range(size)])  4.73 us
    pallas_call x1, Pallas kernels, shards(): pl.pallas_call(krylov_kernel, out_shape=[field] * 4 + [jax.ShapeDtypeStru...  1.32 us
    pallas_call x1, Pallas kernels, shards(): pl.pallas_call(functools.partial(load_kernel, groups), out_shape=[tiles(2...  1.16 us
    pallas_call x1, Pallas kernels, shards(): pl.pallas_call(finish_kernel, out_shape=[field] * 2, in_specs=[vmem] * 6,...  0.87 us
  transfers between devices with their start and end apart: 11, of which 6 were waited for; matrix products, arithmetic and copies ran while one was open for 0% of the time, Pallas kernels for 4%

profile of v3, /device:TPU:0, one launch (start us, length us, event | category | flops | bytes accessed | tf_op | source)
XLA Modules:
  0.0 35.7 jit_solution(17235054254163174196)
XLA Ops:
  0.6 4.1 %collective-permute-start = (bf16[128,128]{1,0:T(8,128)(2,1)}, bf16[128,128]{1,0:T(8,128)(2,1)S(1)}, u32[]{:S(2)}, u32[]{:S(2)}) collective-permute-start(bf16[128,128]{1,0:T(8,128)(2,1)} %block.1), channel_id=1, source_target_pairs={{0,2},{1,3},{2,0},{3,1},{4,6},{5,7},{6,4},{7,5},{8,10},{9,11},{10,... | collective-permute-start | bytes 98312 | tf_op jit(solution)/shard_map/ppermute | solution.py:161
  4.7 1.3 %collective-permute-start.2 = (bf16[128,128]{1,0:T(8,128)(2,1)}, bf16[128,128]{1,0:T(8,128)(2,1)S(1)}, u32[]{:S(2)}, u32[]{:S(2)}) collective-permute-start(bf16[128,128]{1,0:T(8,128)(2,1)} %block.1), channel_id=1, source_target_pairs={{0,3},{1,2},{2,1},{3,0},{4,7},{5,6},{6,5},{7,4},{8,11},{9,10},{10,... | collective-permute-start | bytes 98312 | tf_op jit(solution)/shard_map/ppermute | solution.py:161
  6.1 0.2 collective-permute-start.1
  6.3 1.2 %shard_map.59 = (bf16[4,128,128]{2,1,0:T(8,128)(2,1)S(1)}, bf16[4,128,128]{2,1,0:T(8,128)(2,1)S(1)}, bf16[2,128,128]{2,1,0:T(8,128)(2,1)S(1)}, bf16[4,128,128]{2...) custom-call(bf16[16,128,128]{2,1,0:T(8,128)(2,1)} %confidence.1, ...), custom_call_target="tpu_custom_call" | custom-call | tf_op jit(solution)/shard_map/pallas_call | solution.py:178
  7.5 2.5 %collective-permute-start.8 = (bf16[4,128,128]{2,1,0:T(8,128)(2,1)S(1)}, bf16[4,128,128]{2,1,0:T(8,128)(2,1)S(1)}, u32[]{:S(2)}, u32[]{:S(2)}) collective-permute-start(bf16[4,128,128]{2,1,0:T(8,128)(2,1)S(1)} %get-tuple-element.36), channel_id=1, source_target_pairs={{0,24},{4,28},{8,16},{12,20},{16,8},{20,12},{24,0},{28,4},{1,25},{... | collective-permute-start | bytes 393224 | tf_op jit(solution)/shard_map/ppermute | solution.py:161
  10.0 0.0 collective-permute-done.refs_1_
  10.0 0.7 %collective-permute-done.2.refs_3_ = bf16[128,128]{1,0:T(8,128)(2,1)S(1)} collective-permute-done((bf16[128,128]{1,0:T(8,128)(2,1)}, bf16[128,128]{1,0:T(8,128)(2,1)S(1)}, u32[]{:S(2)}, u32[]{:S(2)}) %collective-permute-start.2) | collective-permute-done | bytes 32800 | tf_op jit(solution)/shard_map/ppermute | solution.py:161
  10.7 0.0 collective-permute-done.1.refs_2_
  10.7 0.3 shard_map.60
  11.0 2.5 %collective-permute-start.3 = (bf16[4,128,128]{2,1,0:T(8,128)(2,1)S(1)}, bf16[4,128,128]{2,1,0:T(8,128)(2,1)S(1)}, u32[]{:S(2)}, u32[]{:S(2)}) collective-permute-start(bf16[4,128,128]{2,1,0:T(8,128)(2,1)S(1)} %get-tuple-element.30), channel_id=1, source_target_pairs={{0,24},{4,28},{8,16},{12,20},{16,8},{20,12},{24,0},{28,4},{1,25},{... | collective-permute-start | bytes 393224 | tf_op jit(solution)/shard_map/ppermute | solution.py:161
  13.5 0.5 %collective-permute-start.4 = (bf16[4,128,128]{2,1,0:T(8,128)(2,1)S(1)}, bf16[4,128,128]{2,1,0:T(8,128)(2,1)S(1)}, u32[]{:S(2)}, u32[]{:S(2)}) collective-permute-start(bf16[4,128,128]{2,1,0:T(8,128)(2,1)S(1)} %get-tuple-element.32), channel_id=1, source_target_pairs={{0,8},{4,12},{8,0},{12,4},{16,24},{20,28},{24,16},{28,20},{1,9},{5... | collective-permute-start | bytes 393224 | tf_op jit(solution)/shard_map/ppermute | solution.py:161
  14.0 0.5 %collective-permute-start.5 = (bf16[4,128,128]{2,1,0:T(8,128)(2,1)S(1)}, bf16[4,128,128]{2,1,0:T(8,128)(2,1)S(1)}, u32[]{:S(2)}, u32[]{:S(2)}) collective-permute-start(bf16[4,128,128]{2,1,0:T(8,128)(2,1)S(1)} %get-tuple-element.33), channel_id=1, source_target_pairs={{0,16},{4,20},{8,24},{12,28},{16,0},{20,4},{24,8},{28,12},{1,17},{... | collective-permute-start | bytes 393224 | tf_op jit(solution)/shard_map/ppermute | solution.py:161
  14.5 0.0 collective-permute-start.6
  14.6 0.0 collective-permute-done.8.far_weights
  14.6 2.7 %collective-permute-start.7 = (bf16[4,128,128]{2,1,0:T(8,128)(2,1)S(1)}, bf16[4,128,128]{2,1,0:T(8,128)(2,1)S(1)}, u32[]{:S(2)}, u32[]{:S(2)}) collective-permute-start(bf16[4,128,128]{2,1,0:T(8,128)(2,1)S(1)} %get-tuple-element.35), channel_id=1, source_target_pairs={{0,12},{4,8},{8,4},{12,0},{16,28},{20,24},{24,20},{28,16},{1,13},{... | collective-permute-start | bytes 393224 | tf_op jit(solution)/shard_map/ppermute | solution.py:161
  17.3 0.3 collective-permute-done.3.far_items
  17.6 0.0 collective-permute-start.9
  17.7 1.9 %collective-permute-done.4.whole_1_ = bf16[4,128,128]{2,1,0:T(8,128)(2,1)S(1)} collective-permute-done((bf16[4,128,128]{2,1,0:T(8,128)(2,1)S(1)}, bf16[4,128,128]{2,1,0:T(8,128)(2,1)S(1)}, u32[]{:S(2)}, u32[]{:S(2)}) %collective-permute-start.4) | collective-permute-done | bytes 131104 | tf_op jit(solution)/shard_map/ppermute | solution.py:161
  19.6 0.0 collective-permute-start.10
  19.6 0.9 %collective-permute-done.5.whole_2_ = bf16[4,128,128]{2,1,0:T(8,128)(2,1)S(1)} collective-permute-done((bf16[4,128,128]{2,1,0:T(8,128)(2,1)S(1)}, bf16[4,128,128]{2,1,0:T(8,128)(2,1)S(1)}, u32[]{:S(2)}, u32[]{:S(2)}) %collective-permute-start.5) | collective-permute-done | bytes 131104 | tf_op jit(solution)/shard_map/ppermute | solution.py:161
  20.4 0.4 %collective-permute-done.6.whole_3_ = bf16[4,128,128]{2,1,0:T(8,128)(2,1)S(1)} collective-permute-done((bf16[4,128,128]{2,1,0:T(8,128)(2,1)S(1)}, bf16[4,128,128]{2,1,0:T(8,128)(2,1)S(1)}, u32[]{:S(2)}, u32[]{:S(2)}) %collective-permute-start.6) | collective-permute-done | bytes 131104 | tf_op jit(solution)/shard_map/ppermute | solution.py:161
  20.9 0.5 %collective-permute-done.7.whole_4_ = bf16[4,128,128]{2,1,0:T(8,128)(2,1)S(1)} collective-permute-done((bf16[4,128,128]{2,1,0:T(8,128)(2,1)S(1)}, bf16[4,128,128]{2,1,0:T(8,128)(2,1)S(1)}, u32[]{:S(2)}, u32[]{:S(2)}) %collective-permute-start.7) | collective-permute-done | bytes 131104 | tf_op jit(solution)/shard_map/ppermute | solution.py:161
  21.4 0.0 collective-permute-done.9.sibling_0_
  21.4 0.0 collective-permute-done.10.sibling_1_
  21.4 1.3 %shard_map.61 = (f32[128,128]{1,0:T(8,128)S(1)}, f32[128,128]{1,0:T(8,128)S(1)}, f32[128,128]{1,0:T(8,128)S(1)}, f32[128,128]{1,0:T(8,128)S(1)}, f32[1,1,128]{2,1,0:T(1,128)S(1)}) custom-call(bf16[4,128,128]{2,1,0:T(8,128)(2,1)S(1)} %collective-permute-done.3.far_items, bf16[4,128,128]{2,1,0:T(8,128)(2,1)S(1)} %get-tuple-element.31.whole_0_, ...), custom_call_target="tpu_custom_call" | custom-call | tf_op jit(solution)/shard_map/pallas_call | solution.py:215
  22.8 12.1 %all_to_all.5 = f32[32,1,1,128]{3,2,1,0:T(1,128)S(1)} all-to-all(f32[32,1,1,128]{3,2,1,0:T(1,128)S(1)} %broadcast_in_dim.9), channel_id=1, replica_groups=mesh['row'=8,'col'=4] {'row','col'}, dimensions={0} | all-to-all | bytes 32768 | tf_op jit(solution)/shard_map/all_to_all | solution.py:146
  34.9 0.9 %shard_map.62 = (f32[128,128]{1,0:T(8,128)}, f32[128,128]{1,0:T(8,128)}) custom-call(f32[32,1,128]{2,1,0:T(1,128)S(1)} %bitcast.2, f32[1,1,128]{2,1,0:T(1,128)S(1)} %get-tuple-element.39.own, f32[128,128]{1,0:T(8,128)S(1)} %get-tuple-element.40.b_ref, f32[128,128]{1,0:T(8,128)S(1)} %get-tuple-element.41.q_ref, f32[128,128]{1,0:T(8,128)S(1)} %get-tuple-element.42.v_ref, ...), custom_call_target="tpu_custom_call" | custom-call | tf_op jit(solution)/shard_map/pallas_call | solution.py:223
  (5 shorter events, 0.0 us)
Async XLA Ops:
  0.6 9.4 %collective-permute-start = (bf16[128,128]{1,0:T(8,128)(2,1)}, bf16[128,128]{1,0:T(8,128)(2,1)S(1)}, u32[]{:S(2)}, u32[]{:S(2)}) collective-permute-start(bf16[128,128]{1,0:T(8,128)(2,1)} %block.1), channel_id=1, source_target_pairs={{0,2},{1,3},{2,0},{3,1},{4,6},{5,7},{6,4},{7,5},{8,10},{9,11},{10,... | collective-permute-start | bytes 98312 | tf_op jit(solution)/shard_map/ppermute | solution.py:161
  4.7 5.9 %collective-permute-start.2 = (bf16[128,128]{1,0:T(8,128)(2,1)}, bf16[128,128]{1,0:T(8,128)(2,1)S(1)}, u32[]{:S(2)}, u32[]{:S(2)}) collective-permute-start(bf16[128,128]{1,0:T(8,128)(2,1)} %block.1), channel_id=1, source_target_pairs={{0,3},{1,2},{2,1},{3,0},{4,7},{5,6},{6,5},{7,4},{8,11},{9,10},{10,... | collective-permute-start | bytes 98312 | tf_op jit(solution)/shard_map/ppermute | solution.py:161
  6.1 4.6 %collective-permute-start.1 = (bf16[128,128]{1,0:T(8,128)(2,1)}, bf16[128,128]{1,0:T(8,128)(2,1)S(1)}, u32[]{:S(2)}, u32[]{:S(2)}) collective-permute-start(bf16[128,128]{1,0:T(8,128)(2,1)} %block.1), channel_id=1, source_target_pairs={{0,1},{1,0},{2,3},{3,2},{4,5},{5,4},{6,7},{7,6},{8,9},{9,8},{10,11... | collective-permute-start | bytes 98312 | tf_op jit(solution)/shard_map/ppermute | solution.py:161
  7.5 7.1 %collective-permute-start.8 = (bf16[4,128,128]{2,1,0:T(8,128)(2,1)S(1)}, bf16[4,128,128]{2,1,0:T(8,128)(2,1)S(1)}, u32[]{:S(2)}, u32[]{:S(2)}) collective-permute-start(bf16[4,128,128]{2,1,0:T(8,128)(2,1)S(1)} %get-tuple-element.36), channel_id=1, source_target_pairs={{0,24},{4,28},{8,16},{12,20},{16,8},{20,12},{24,0},{28,4},{1,25},{... | collective-permute-start | bytes 393224 | tf_op jit(solution)/shard_map/ppermute | solution.py:161
  11.0 6.6 %collective-permute-start.3 = (bf16[4,128,128]{2,1,0:T(8,128)(2,1)S(1)}, bf16[4,128,128]{2,1,0:T(8,128)(2,1)S(1)}, u32[]{:S(2)}, u32[]{:S(2)}) collective-permute-start(bf16[4,128,128]{2,1,0:T(8,128)(2,1)S(1)} %get-tuple-element.30), channel_id=1, source_target_pairs={{0,24},{4,28},{8,16},{12,20},{16,8},{20,12},{24,0},{28,4},{1,25},{... | collective-permute-start | bytes 393224 | tf_op jit(solution)/shard_map/ppermute | solution.py:161
  13.5 6.1 %collective-permute-start.4 = (bf16[4,128,128]{2,1,0:T(8,128)(2,1)S(1)}, bf16[4,128,128]{2,1,0:T(8,128)(2,1)S(1)}, u32[]{:S(2)}, u32[]{:S(2)}) collective-permute-start(bf16[4,128,128]{2,1,0:T(8,128)(2,1)S(1)} %get-tuple-element.32), channel_id=1, source_target_pairs={{0,8},{4,12},{8,0},{12,4},{16,24},{20,28},{24,16},{28,20},{1,9},{5... | collective-permute-start | bytes 393224 | tf_op jit(solution)/shard_map/ppermute | solution.py:161
  14.0 6.4 %collective-permute-start.5 = (bf16[4,128,128]{2,1,0:T(8,128)(2,1)S(1)}, bf16[4,128,128]{2,1,0:T(8,128)(2,1)S(1)}, u32[]{:S(2)}, u32[]{:S(2)}) collective-permute-start(bf16[4,128,128]{2,1,0:T(8,128)(2,1)S(1)} %get-tuple-element.33), channel_id=1, source_target_pairs={{0,16},{4,20},{8,24},{12,28},{16,0},{20,4},{24,8},{28,12},{1,17},{... | collective-permute-start | bytes 393224 | tf_op jit(solution)/shard_map/ppermute | solution.py:161
  14.5 6.3 %collective-permute-start.6 = (bf16[4,128,128]{2,1,0:T(8,128)(2,1)S(1)}, bf16[4,128,128]{2,1,0:T(8,128)(2,1)S(1)}, u32[]{:S(2)}, u32[]{:S(2)}) collective-permute-start(bf16[4,128,128]{2,1,0:T(8,128)(2,1)S(1)} %get-tuple-element.34), channel_id=1, source_target_pairs={{0,20},{4,16},{8,28},{12,24},{16,4},{20,0},{24,12},{28,8},{1,21},{... | collective-permute-start | bytes 393224 | tf_op jit(solution)/shard_map/ppermute | solution.py:161
  14.6 6.8 %collective-permute-start.7 = (bf16[4,128,128]{2,1,0:T(8,128)(2,1)S(1)}, bf16[4,128,128]{2,1,0:T(8,128)(2,1)S(1)}, u32[]{:S(2)}, u32[]{:S(2)}) collective-permute-start(bf16[4,128,128]{2,1,0:T(8,128)(2,1)S(1)} %get-tuple-element.35), channel_id=1, source_target_pairs={{0,12},{4,8},{8,4},{12,0},{16,28},{20,24},{24,20},{28,16},{1,13},{... | collective-permute-start | bytes 393224 | tf_op jit(solution)/shard_map/ppermute | solution.py:161
  17.6 3.8 %collective-permute-start.9 = (bf16[4,128,128]{2,1,0:T(8,128)(2,1)S(1)}, bf16[4,128,128]{2,1,0:T(8,128)(2,1)S(1)}, u32[]{:S(2)}, u32[]{:S(2)}) collective-permute-start(bf16[4,128,128]{2,1,0:T(8,128)(2,1)S(1)} %pad_maximum_fusion), channel_id=1, source_target_pairs={{0,4},{4,0},{8,12},{12,8},{16,20},{20,16},{24,28},{28,24},{1,5},{5... | collective-permute-start | bytes 393224 | tf_op jit(solution)/shard_map/ppermute | solution.py:161
  19.6 1.8 %collective-permute-start.10 = (bf16[4,128,128]{2,1,0:T(8,128)(2,1)S(1)}, bf16[4,128,128]{2,1,0:T(8,128)(2,1)S(1)}, u32[]{:S(2)}, u32[]{:S(2)}) collective-permute-start(bf16[4,128,128]{2,1,0:T(8,128)(2,1)S(1)} %pad_maximum_fusion.1), channel_id=1, source_target_pairs={{0,4},{4,0},{8,12},{12,8},{16,20},{20,16},{24,28},{28,24},{1,5},{5... | collective-permute-start | bytes 393224 | tf_op jit(solution)/shard_map/ppermute | solution.py:161

commit v4 on v3

--- a/solution.py
+++ b/solution.py
@@ -27,7 +27,7 @@
     cols = marks.shape[1]
     row, col = lax.axis_index("row"), lax.axis_index("col")
     pairs = [(item_blocks, blocks_here), (counts, counts_here)]
-    targets = [(groups - 2, far, 0), (groups - 1, far, per_owner)]
+    targets = [(groups - 1, far, 0), (groups - 2, far, per_owner)]
     targets += [(shift, parcel, 0) for shift, parcel in enumerate(parcels)]
     pairs += [
         (confidence.at[pl.ds((row ^ shift) * per_owner, per_owner)], target.at[pl.ds(first, per_owner)])
@@ -56,7 +56,7 @@
         slab[shift] = block[...]
     per_owner = marks.shape[0] // groups
     rows = marks.shape[2]
-    targets = [(groups - 2, far, 0), (groups - 1, far, per_owner), (1, sibling, 0)]
+    targets = [(groups - 1, far, 0), (groups - 2, far, per_owner), (1, sibling, 0)]
     targets += [(shift, parcel, per_owner) for shift, parcel in zip(late, parcels)]
     for shift, target, first in targets:
         for place in range(per_owner):
@@ -173,17 +173,17 @@
     def tiles(count):
         return jax.ShapeDtypeStruct((count, width, factor_width), item_factors.dtype)
 
-    far = groups - 2
+    far = groups - 1
     cols = lax.axis_size("col")
     early, *loaded, marks, block_here = pl.pallas_call(
         functools.partial(load_kernel, groups),
-        out_shape=[tiles(2 * per_owner if shift != 1 else per_owner) for shift in [far, *range(far)]]
+        out_shape=[tiles(2 * per_owner if shift != 1 else per_owner) for shift in [far, *range(groups - 2)]]
         + [
             jax.ShapeDtypeStruct((slots, cols, 16, factor_width), item_factors.dtype),
             jax.ShapeDtypeStruct(item_factors.shape, item_factors.dtype),
         ],
         in_specs=[pl.BlockSpec(memory_space=pl.ANY)] * 4,
-        out_specs=[vmem] * (far + 3),
+        out_specs=[vmem] * (groups + 1),
         scratch_shapes=[
             pltpu.SMEM(item_blocks.shape, item_blocks.dtype),
             pltpu.SMEM(counts.shape, counts.dtype),

time: 35.9 us -> 36.4 us (1.014)
  waiting for transfers between devices: 4.73 us -> 7.92 us
  blocking collectives: 12.1 us -> 10.6 us
  starting transfers between devices: 14.5 us -> 13.3 us
    ppermute x11, waiting for transfers between devices: 4.73 us -> 7.92 us  [swap(): lax.ppermute(block, axis, [(i, i ^ shift) for i in range(size)])]
    all_to_all x1, blocking collectives: 12.1 us -> 10.6 us  [everyone(): lax.all_to_all(copies, axes, split_axis=0, concat_axis=0, tiled=True)]
    ppermute x11, starting transfers between devices: 14.5 us -> 13.3 us  [swap(): lax.ppermute(block, axis, [(i, i ^ shift) for i in range(size)])]
  transfers between devices with their start and end apart: 11 -> 11, of which waited for: 6 -> 4; matrix products, arithmetic and copies ran while one was open for 0% -> 0% of each run, Pallas kernels for 4% -> 4%
where the time goes in v4:
time: 36.4 us; the launch traced here: 36.2 us
  starting transfers between devices  13.3 us (37%)
  blocking collectives  10.6 us (29%)
  waiting for transfers between devices  7.92 us (22%)
  Pallas kernels  3.68 us (10%)
  between operations  0.68 us (2%)
    ppermute x11, starting transfers between devices, swap(): lax.ppermute(block, axis, [(i, i ^ shift) for i in range(size)])  13.3 us
    all_to_all x1, blocking collectives, everyone(): lax.all_to_all(copies, axes, split_axis=0, concat_axis=0, tiled=True)  10.6 us
    ppermute x11, waiting for transfers between devices, swap(): lax.ppermute(block, axis, [(i, i ^ shift) for i in range(size)])  7.92 us
    pallas_call x1, Pallas kernels, shards(): pl.pallas_call(krylov_kernel, out_shape=[field] * 4 + [jax.ShapeDtypeStru...  1.32 us
    pallas_call x1, Pallas kernels, shards(): pl.pallas_call(functools.partial(load_kernel, groups), out_shape=[tiles(2...  1.16 us
    pallas_call x1, Pallas kernels, shards(): pl.pallas_call(finish_kernel, out_shape=[field] * 2, in_specs=[vmem] * 6,...  0.87 us
  transfers between devices with their start and end apart: 11, of which 4 were waited for; matrix products, arithmetic and copies ran while one was open for 0% of the time, Pallas kernels for 4%

profile of v4, /device:TPU:0, one launch (start us, length us, event | category | flops | bytes accessed | tf_op | source)
XLA Modules:
  0.0 36.2 jit_solution(13212438969180456294)
XLA Ops:
  0.6 4.1 %collective-permute-start = (bf16[128,128]{1,0:T(8,128)(2,1)}, bf16[128,128]{1,0:T(8,128)(2,1)S(1)}, u32[]{:S(2)}, u32[]{:S(2)}) collective-permute-start(bf16[128,128]{1,0:T(8,128)(2,1)} %block.1), channel_id=1, source_target_pairs={{0,2},{1,3},{2,0},{3,1},{4,6},{5,7},{6,4},{7,5},{8,10},{9,11},{10,... | collective-permute-start | bytes 98312 | tf_op jit(solution)/shard_map/ppermute | solution.py:161
  4.7 1.3 %collective-permute-start.2 = (bf16[128,128]{1,0:T(8,128)(2,1)}, bf16[128,128]{1,0:T(8,128)(2,1)S(1)}, u32[]{:S(2)}, u32[]{:S(2)}) collective-permute-start(bf16[128,128]{1,0:T(8,128)(2,1)} %block.1), channel_id=1, source_target_pairs={{0,3},{1,2},{2,1},{3,0},{4,7},{5,6},{6,5},{7,4},{8,11},{9,10},{10,... | collective-permute-start | bytes 98312 | tf_op jit(solution)/shard_map/ppermute | solution.py:161
  6.1 0.2 collective-permute-start.1
  6.3 1.2 %shard_map.59 = (bf16[4,128,128]{2,1,0:T(8,128)(2,1)S(1)}, bf16[4,128,128]{2,1,0:T(8,128)(2,1)S(1)}, bf16[2,128,128]{2,1,0:T(8,128)(2,1)S(1)}, bf16[4,128,128]{2...) custom-call(bf16[16,128,128]{2,1,0:T(8,128)(2,1)} %confidence.1, ...), custom_call_target="tpu_custom_call" | custom-call | tf_op jit(solution)/shard_map/pallas_call | solution.py:178
  7.5 1.4 %collective-permute-start.8 = (bf16[4,128,128]{2,1,0:T(8,128)(2,1)S(1)}, bf16[4,128,128]{2,1,0:T(8,128)(2,1)S(1)}, u32[]{:S(2)}, u32[]{:S(2)}) collective-permute-start(bf16[4,128,128]{2,1,0:T(8,128)(2,1)S(1)} %get-tuple-element.36), channel_id=1, source_target_pairs={{0,28},{4,24},{8,20},{12,16},{16,12},{20,8},{24,4},{28,0},{1,29},{... | collective-permute-start | bytes 393224 | tf_op jit(solution)/shard_map/ppermute | solution.py:161
  8.9 0.0 collective-permute-done.refs_1_
  8.9 1.8 %collective-permute-done.2.refs_3_ = bf16[128,128]{1,0:T(8,128)(2,1)S(1)} collective-permute-done((bf16[128,128]{1,0:T(8,128)(2,1)}, bf16[128,128]{1,0:T(8,128)(2,1)S(1)}, u32[]{:S(2)}, u32[]{:S(2)}) %collective-permute-start.2) | collective-permute-done | bytes 32800 | tf_op jit(solution)/shard_map/ppermute | solution.py:161
  10.7 0.0 collective-permute-done.1.refs_2_
  10.7 0.3 shard_map.60
  11.0 0.5 %collective-permute-start.3 = (bf16[4,128,128]{2,1,0:T(8,128)(2,1)S(1)}, bf16[4,128,128]{2,1,0:T(8,128)(2,1)S(1)}, u32[]{:S(2)}, u32[]{:S(2)}) collective-permute-start(bf16[4,128,128]{2,1,0:T(8,128)(2,1)S(1)} %get-tuple-element.30), channel_id=1, source_target_pairs={{0,28},{4,24},{8,20},{12,16},{16,12},{20,8},{24,4},{28,0},{1,29},{... | collective-permute-start | bytes 393224 | tf_op jit(solution)/shard_map/ppermute | solution.py:161
  11.5 1.1 %collective-permute-start.4 = (bf16[4,128,128]{2,1,0:T(8,128)(2,1)S(1)}, bf16[4,128,128]{2,1,0:T(8,128)(2,1)S(1)}, u32[]{:S(2)}, u32[]{:S(2)}) collective-permute-start(bf16[4,128,128]{2,1,0:T(8,128)(2,1)S(1)} %get-tuple-element.32), channel_id=1, source_target_pairs={{0,8},{4,12},{8,0},{12,4},{16,24},{20,28},{24,16},{28,20},{1,9},{5... | collective-permute-start | bytes 393224 | tf_op jit(solution)/shard_map/ppermute | solution.py:161
  12.6 1.5 %collective-permute-start.5 = (bf16[4,128,128]{2,1,0:T(8,128)(2,1)S(1)}, bf16[4,128,128]{2,1,0:T(8,128)(2,1)S(1)}, u32[]{:S(2)}, u32[]{:S(2)}) collective-permute-start(bf16[4,128,128]{2,1,0:T(8,128)(2,1)S(1)} %get-tuple-element.33), channel_id=1, source_target_pairs={{0,16},{4,20},{8,24},{12,28},{16,0},{20,4},{24,8},{28,12},{1,17},{... | collective-permute-start | bytes 393224 | tf_op jit(solution)/shard_map/ppermute | solution.py:161
  14.2 1.1 %collective-permute-start.6 = (bf16[4,128,128]{2,1,0:T(8,128)(2,1)S(1)}, bf16[4,128,128]{2,1,0:T(8,128)(2,1)S(1)}, u32[]{:S(2)}, u32[]{:S(2)}) collective-permute-start(bf16[4,128,128]{2,1,0:T(8,128)(2,1)S(1)} %get-tuple-element.34), channel_id=1, source_target_pairs={{0,20},{4,16},{8,28},{12,24},{16,4},{20,0},{24,12},{28,8},{1,21},{... | collective-permute-start | bytes 393224 | tf_op jit(solution)/shard_map/ppermute | solution.py:161
  15.2 0.0 collective-permute-done.8.far_weights
  15.2 0.1 collective-permute-start.7
  15.3 2.4 %collective-permute-done.3.far_items = bf16[4,128,128]{2,1,0:T(8,128)(2,1)S(1)} collective-permute-done((bf16[4,128,128]{2,1,0:T(8,128)(2,1)S(1)}, bf16[4,128,128]{2,1,0:T(8,128)(2,1)S(1)}, u32[]{:S(2)}, u32[]{:S(2)}) %collective-permute-start.3) | collective-permute-done | bytes 131104 | tf_op jit(solution)/shard_map/ppermute | solution.py:161
  17.8 0.0 collective-permute-start.9
  17.8 1.0 %collective-permute-done.4.whole_1_ = bf16[4,128,128]{2,1,0:T(8,128)(2,1)S(1)} collective-permute-done((bf16[4,128,128]{2,1,0:T(8,128)(2,1)S(1)}, bf16[4,128,128]{2,1,0:T(8,128)(2,1)S(1)}, u32[]{:S(2)}, u32[]{:S(2)}) %collective-permute-start.4) | collective-permute-done | bytes 131104 | tf_op jit(solution)/shard_map/ppermute | solution.py:161
  18.8 1.9 %collective-permute-start.10 = (bf16[4,128,128]{2,1,0:T(8,128)(2,1)S(1)}, bf16[4,128,128]{2,1,0:T(8,128)(2,1)S(1)}, u32[]{:S(2)}, u32[]{:S(2)}) collective-permute-start(bf16[4,128,128]{2,1,0:T(8,128)(2,1)S(1)} %pad_maximum_fusion.1), channel_id=1, source_target_pairs={{0,4},{4,0},{8,12},{12,8},{16,20},{20,16},{24,28},{28,24},{1,5},{5... | collective-permute-start | bytes 393224 | tf_op jit(solution)/shard_map/ppermute | solution.py:161
  20.7 0.0 collective-permute-done.5.whole_2_
  20.7 2.7 %collective-permute-done.6.whole_3_ = bf16[4,128,128]{2,1,0:T(8,128)(2,1)S(1)} collective-permute-done((bf16[4,128,128]{2,1,0:T(8,128)(2,1)S(1)}, bf16[4,128,128]{2,1,0:T(8,128)(2,1)S(1)}, u32[]{:S(2)}, u32[]{:S(2)}) %collective-permute-start.6) | collective-permute-done | bytes 131104 | tf_op jit(solution)/shard_map/ppermute | solution.py:161
  23.4 0.0 collective-permute-done.7.whole_4_
  23.4 0.0 collective-permute-done.9.sibling_0_
  23.4 0.0 collective-permute-done.10.sibling_1_
  23.4 1.3 %shard_map.61 = (f32[128,128]{1,0:T(8,128)S(1)}, f32[128,128]{1,0:T(8,128)S(1)}, f32[128,128]{1,0:T(8,128)S(1)}, f32[128,128]{1,0:T(8,128)S(1)}, f32[1,1,128]{2,1,0:T(1,128)S(1)}) custom-call(bf16[4,128,128]{2,1,0:T(8,128)(2,1)S(1)} %collective-permute-done.3.far_items, bf16[4,128,128]{2,1,0:T(8,128)(2,1)S(1)} %get-tuple-element.31.whole_0_, ...), custom_call_target="tpu_custom_call" | custom-call | tf_op jit(solution)/shard_map/pallas_call | solution.py:215
  24.7 10.6 %all_to_all.5 = f32[32,1,1,128]{3,2,1,0:T(1,128)S(1)} all-to-all(f32[32,1,1,128]{3,2,1,0:T(1,128)S(1)} %broadcast_in_dim.9), channel_id=1, replica_groups=mesh['row'=8,'col'=4] {'row','col'}, dimensions={0} | all-to-all | bytes 32768 | tf_op jit(solution)/shard_map/all_to_all | solution.py:146
  35.3 0.9 %shard_map.62 = (f32[128,128]{1,0:T(8,128)}, f32[128,128]{1,0:T(8,128)}) custom-call(f32[32,1,128]{2,1,0:T(1,128)S(1)} %bitcast.2, f32[1,1,128]{2,1,0:T(1,128)S(1)} %get-tuple-element.39.own, f32[128,128]{1,0:T(8,128)S(1)} %get-tuple-element.40.b_ref, f32[128,128]{1,0:T(8,128)S(1)} %get-tuple-element.41.q_ref, f32[128,128]{1,0:T(8,128)S(1)} %get-tuple-element.42.v_ref, ...), custom_call_target="tpu_custom_call" | custom-call | tf_op jit(solution)/shard_map/pallas_call | solution.py:223
  (5 shorter events, 0.0 us)
Async XLA Ops:
  0.6 8.2 %collective-permute-start = (bf16[128,128]{1,0:T(8,128)(2,1)}, bf16[128,128]{1,0:T(8,128)(2,1)S(1)}, u32[]{:S(2)}, u32[]{:S(2)}) collective-permute-start(bf16[128,128]{1,0:T(8,128)(2,1)} %block.1), channel_id=1, source_target_pairs={{0,2},{1,3},{2,0},{3,1},{4,6},{5,7},{6,4},{7,5},{8,10},{9,11},{10,... | collective-permute-start | bytes 98312 | tf_op jit(solution)/shard_map/ppermute | solution.py:161
  4.7 5.9 %collective-permute-start.2 = (bf16[128,128]{1,0:T(8,128)(2,1)}, bf16[128,128]{1,0:T(8,128)(2,1)S(1)}, u32[]{:S(2)}, u32[]{:S(2)}) collective-permute-start(bf16[128,128]{1,0:T(8,128)(2,1)} %block.1), channel_id=1, source_target_pairs={{0,3},{1,2},{2,1},{3,0},{4,7},{5,6},{6,5},{7,4},{8,11},{9,10},{10,... | collective-permute-start | bytes 98312 | tf_op jit(solution)/shard_map/ppermute | solution.py:161
  6.1 4.6 %collective-permute-start.1 = (bf16[128,128]{1,0:T(8,128)(2,1)}, bf16[128,128]{1,0:T(8,128)(2,1)S(1)}, u32[]{:S(2)}, u32[]{:S(2)}) collective-permute-start(bf16[128,128]{1,0:T(8,128)(2,1)} %block.1), channel_id=1, source_target_pairs={{0,1},{1,0},{2,3},{3,2},{4,5},{5,4},{6,7},{7,6},{8,9},{9,8},{10,11... | collective-permute-start | bytes 98312 | tf_op jit(solution)/shard_map/ppermute | solution.py:161
  7.5 7.8 %collective-permute-start.8 = (bf16[4,128,128]{2,1,0:T(8,128)(2,1)S(1)}, bf16[4,128,128]{2,1,0:T(8,128)(2,1)S(1)}, u32[]{:S(2)}, u32[]{:S(2)}) collective-permute-start(bf16[4,128,128]{2,1,0:T(8,128)(2,1)S(1)} %get-tuple-element.36), channel_id=1, source_target_pairs={{0,28},{4,24},{8,20},{12,16},{16,12},{20,8},{24,4},{28,0},{1,29},{... | collective-permute-start | bytes 393224 | tf_op jit(solution)/shard_map/ppermute | solution.py:161
  11.0 6.8 %collective-permute-start.3 = (bf16[4,128,128]{2,1,0:T(8,128)(2,1)S(1)}, bf16[4,128,128]{2,1,0:T(8,128)(2,1)S(1)}, u32[]{:S(2)}, u32[]{:S(2)}) collective-permute-start(bf16[4,128,128]{2,1,0:T(8,128)(2,1)S(1)} %get-tuple-element.30), channel_id=1, source_target_pairs={{0,28},{4,24},{8,20},{12,16},{16,12},{20,8},{24,4},{28,0},{1,29},{... | collective-permute-start | bytes 393224 | tf_op jit(solution)/shard_map/ppermute | solution.py:161
  11.5 7.3 %collective-permute-start.4 = (bf16[4,128,128]{2,1,0:T(8,128)(2,1)S(1)}, bf16[4,128,128]{2,1,0:T(8,128)(2,1)S(1)}, u32[]{:S(2)}, u32[]{:S(2)}) collective-permute-start(bf16[4,128,128]{2,1,0:T(8,128)(2,1)S(1)} %get-tuple-element.32), channel_id=1, source_target_pairs={{0,8},{4,12},{8,0},{12,4},{16,24},{20,28},{24,16},{28,20},{1,9},{5... | collective-permute-start | bytes 393224 | tf_op jit(solution)/shard_map/ppermute | solution.py:161
  12.6 8.1 %collective-permute-start.5 = (bf16[4,128,128]{2,1,0:T(8,128)(2,1)S(1)}, bf16[4,128,128]{2,1,0:T(8,128)(2,1)S(1)}, u32[]{:S(2)}, u32[]{:S(2)}) collective-permute-start(bf16[4,128,128]{2,1,0:T(8,128)(2,1)S(1)} %get-tuple-element.33), channel_id=1, source_target_pairs={{0,16},{4,20},{8,24},{12,28},{16,0},{20,4},{24,8},{28,12},{1,17},{... | collective-permute-start | bytes 393224 | tf_op jit(solution)/shard_map/ppermute | solution.py:161
  14.2 9.2 %collective-permute-start.6 = (bf16[4,128,128]{2,1,0:T(8,128)(2,1)S(1)}, bf16[4,128,128]{2,1,0:T(8,128)(2,1)S(1)}, u32[]{:S(2)}, u32[]{:S(2)}) collective-permute-start(bf16[4,128,128]{2,1,0:T(8,128)(2,1)S(1)} %get-tuple-element.34), channel_id=1, source_target_pairs={{0,20},{4,16},{8,28},{12,24},{16,4},{20,0},{24,12},{28,8},{1,21},{... | collective-permute-start | bytes 393224 | tf_op jit(solution)/shard_map/ppermute | solution.py:161
  15.2 8.1 %collective-permute-start.7 = (bf16[4,128,128]{2,1,0:T(8,128)(2,1)S(1)}, bf16[4,128,128]{2,1,0:T(8,128)(2,1)S(1)}, u32[]{:S(2)}, u32[]{:S(2)}) collective-permute-start(bf16[4,128,128]{2,1,0:T(8,128)(2,1)S(1)} %get-tuple-element.35), channel_id=1, source_target_pairs={{0,12},{4,8},{8,4},{12,0},{16,28},{20,24},{24,20},{28,16},{1,13},{... | collective-permute-start | bytes 393224 | tf_op jit(solution)/shard_map/ppermute | solution.py:161
  17.8 5.6 %collective-permute-start.9 = (bf16[4,128,128]{2,1,0:T(8,128)(2,1)S(1)}, bf16[4,128,128]{2,1,0:T(8,128)(2,1)S(1)}, u32[]{:S(2)}, u32[]{:S(2)}) collective-permute-start(bf16[4,128,128]{2,1,0:T(8,128)(2,1)S(1)} %pad_maximum_fusion), channel_id=1, source_target_pairs={{0,4},{4,0},{8,12},{12,8},{16,20},{20,16},{24,28},{28,24},{1,5},{5... | collective-permute-start | bytes 393224 | tf_op jit(solution)/shard_map/ppermute | solution.py:161
  18.8 4.6 %collective-permute-start.10 = (bf16[4,128,128]{2,1,0:T(8,128)(2,1)S(1)}, bf16[4,128,128]{2,1,0:T(8,128)(2,1)S(1)}, u32[]{:S(2)}, u32[]{:S(2)}) collective-permute-start(bf16[4,128,128]{2,1,0:T(8,128)(2,1)S(1)} %pad_maximum_fusion.1), channel_id=1, source_target_pairs={{0,4},{4,0},{8,12},{12,8},{16,20},{20,16},{24,28},{28,24},{1,5},{5... | collective-permute-start | bytes 393224 | tf_op jit(solution)/shard_map/ppermute | solution.py:161
